TPU v7x, 256 devices: a whole 4x4x8 slice. The times are simulated.
256 devices in a mesh: section: 32 (over z, x), tensor: 8 (over y, core).
Axes of the slice: x: 4, y: 4, z: 8, core: 2. Of those that a mesh axis runs over, the one named last changes fastest.
Arguments:
- hidden: bfloat16 [512, 4608], P('section'), may hold values from -16 to 16
- head_weight: bfloat16 [2048, 64, 4608], P('section', 'tensor'), may hold values from -0.3 to 0.3
- panel_section: int32 [2048, 1], replicated, may hold values from 0 to 31; in each aligned block of 64 rows (0 to 63, 64 to 127, ...) at most 2 rows name the same one
- targets: int32 [512], replicated, may hold values from 0 to 131071
Outputs:
- loss: float32 [512], P('section')
- hidden_grad: float32 [512, 4608], P(('section', 'tensor'))
- slot_grads: bfloat16 [32, 32, 2, 64, 4608], P('section', None, None, 'tensor')
Inputs may be any that keep to these rules, and one draw needn't show every extreme that they name: `panel_section`: among the 64 panels of one home section, each section is assigned at most 2 of them, and in every draw some home assigns exactly 2 to one section.
All inputs are finite; a program needn't handle non-finite values.
Results may differ from a plain program's by a relative error of at most 0.009.
Values may be sent and summed in bfloat16 or wider, within the bound.
A program may use at most 128 MiB of HBM per device.

v0:
```python
import jax
import jax.numpy as jnp
from jax import lax
from jax.sharding import PartitionSpec as P


def home_ranks(dest):
    count = dest.shape[1]
    same = dest[:, :, None] == dest[:, None, :]
    order = jnp.arange(count, dtype=jnp.int32)
    earlier = order[None, :] < order[:, None]
    return jnp.sum((same & earlier[None]).astype(jnp.int32), axis=2)


def softmax_grad(logits, col_ids, live_cols, targets):
    masked = jnp.where(live_cols[None, :], logits, -1e30)
    hits = (col_ids[None, :] == targets[:, None]) & live_cols[None, :]
    local_target = jnp.sum(jnp.where(hits, logits, 0.0), axis=1)
    top = lax.pmax(jnp.max(masked, axis=1), ("section", "tensor"))
    shifted = jnp.where(live_cols[None, :], jnp.exp(masked - top[:, None]), 0.0)
    total, picked = lax.psum((jnp.sum(shifted, axis=1), local_target), ("section", "tensor"))
    loss = jnp.log(total) + top - picked
    dlogits = (shifted / total[:, None] - hits.astype(jnp.float32)).astype(jnp.bfloat16)
    return (loss, dlogits)


def on_device(hidden, head_weight, panel_section, targets):
    sections = lax.axis_size("section")
    tensors = lax.axis_size("tensor")
    myself = lax.axis_index("section")
    portion = lax.axis_index("tensor")
    per_section, rows, width = head_weight.shape
    slots = 5 * per_section // (4 * sections)
    panel_rows = rows * tensors
    dest = panel_section[:, 0].reshape(sections, per_section)
    ranks = home_ranks(dest)
    my_dest = lax.dynamic_index_in_dim(dest, myself, 0, keepdims=False)
    my_rank = lax.dynamic_index_in_dim(ranks, myself, 0, keepdims=False)
    section_ids = jnp.arange(sections, dtype=jnp.int32)
    slot_ids = jnp.arange(slots, dtype=jnp.int32)
    send_map = (
        (my_dest[None, None, :] == section_ids[:, None, None])
        & (my_rank[None, None, :] == slot_ids[None, :, None])
    ).astype(jnp.bfloat16)
    whole = lax.all_gather(hidden, "section", axis=0, tiled=True)
    row_ids = jnp.arange(rows, dtype=jnp.int32)
    packed = jnp.einsum(
        "dkj,jx->dkx",
        send_map,
        head_weight.reshape(per_section, rows * width),
        preferred_element_type=jnp.float32,
    ).astype(jnp.bfloat16)
    arrived = lax.all_to_all(packed, "section", split_axis=0, concat_axis=0, tiled=True)
    match = (dest[:, None, :] == myself) & (ranks[:, None, :] == slot_ids[None, :, None])
    homes = section_ids[:, None] * per_section + jnp.arange(per_section, dtype=jnp.int32)[None, :]
    panel_ids = jnp.sum(jnp.where(match, homes[:, None, :], 0), axis=2)
    live = jnp.any(match, axis=2)
    panels = arrived.reshape(sections * slots * rows, width)
    col_ids = (
        (panel_ids * panel_rows + portion * rows)[:, :, None] + row_ids[None, None, :]
    ).reshape(-1)
    live_cols = jnp.broadcast_to(live[:, :, None], (sections, slots, rows)).reshape(-1)
    logits = lax.dot_general(
        whole, panels, (((1,), (1,)), ((), ())), preferred_element_type=jnp.float32
    )
    loss, dlogits = softmax_grad(logits, col_ids, live_cols, targets)
    partial_grad = jnp.dot(dlogits, panels, preferred_element_type=jnp.float32)
    hidden_grad = lax.psum_scatter(
        partial_grad, ("section", "tensor"), scatter_dimension=0, tiled=True
    )
    grads = lax.dot_general(
        dlogits, whole, (((0,), (0,)), ((), ())), preferred_element_type=jnp.float32
    ).astype(jnp.bfloat16)
    slot_grads = grads.reshape(1, sections, slots, rows, width)
    own_rows = hidden.shape[0]
    own_loss = lax.dynamic_slice_in_dim(loss, myself * own_rows, own_rows)
    return (own_loss, hidden_grad, slot_grads)


def solution(mesh):
    in_specs = (P("section", None), P("section", "tensor", None), P(), P())
    out_specs = (
        P("section"),
        P(("section", "tensor"), None),
        P("section", None, None, "tensor", None),
    )
    return jax.shard_map(
        on_device, mesh=mesh, in_specs=in_specs, out_specs=out_specs, check_vma=False
    )
```

profile of v0, /device:TPU:1, one launch (start us, length us, event | category | flops | bytes accessed | tf_op | source)
XLA Modules:
  0.0 631.4 jit_solution(15093848678762168386)
XLA Ops:
  7.2 0.5 broadcast.72
  7.7 1.4 reduce.3
  9.1 0.9 convert_reduce_fusion
  10.1 7.7 %reshape.134 = bf16[64,36864,1]{1,0,2:T(8,128)(2,1)} reshape(bf16[64,8,4608]{2,1,0:T(8,128)(2,1)} %param.5) | data formatting | bytes 9437184 | tf_op jit(solution)/shard_map/reshape | solution.py:50
  17.8 5.8 convolution_convert_fusion
  23.7 9.4 %copy.10 = bf16[32,2,36864]{2,1,0:T(2,128)(2,1)} copy(bf16[32,2,36864]{2,0,1:T(8,128)(2,1)} %convolution_convert_fusion) | data formatting | bytes 9437184 | tf_op jit(solution)/shard_map/convert_element_type | solution.py:52
  33.0 12.0 %all-to-all-start = ((bf16[32,2,36864]{2,1,0:T(2,128)(2,1)}), bf16[32,2,36864]{2,1,0:T(2,128)(2,1)}, u32[]{:S(2)}, u32[]{:S(2)}) async-start(bf16[32,2,36864]{2,1,0:T(2,128)(2,1)} %copy.10), calls=%async_computation | async-start | bytes 9437184 | tf_op jit(solution)/shard_map/all_to_all | solution.py:53
  45.1 0.7 all-gather.2.cloned.1.call-update
  45.8 0.1 fusion.2
  45.9 0.1 copy.9
  46.0 0.1 broadcast_in_dim.35
  46.3 0.1 select_reduce_fusion.2
  46.7 0.1 add.74
  46.8 124.3 %all-to-all-done = bf16[32,2,36864]{2,1,0:T(2,128)(2,1)} async-done(((bf16[32,2,36864]{2,1,0:T(2,128)(2,1)}), bf16[32,2,36864]{2,1,0:T(2,128)(2,1)}, u32[]{:S(2)}, u32[]{:S(2)}) %all-to-all-start) | async-done | bytes 4718624 | tf_op jit(solution)/shard_map/all_to_all | solution.py:53
  171.1 8.3 %reshape.132 = bf16[512,4608]{1,0:T(8,128)(2,1)} reshape(bf16[32,2,36864]{2,1,0:T(2,128)(2,1)} %all-to-all-done) | data formatting | bytes 9437184 | tf_op jit(solution)/shard_map/reshape | solution.py:58
  179.4 6.2 select_reduce_fusion.1
  185.6 80.3 %pmax.7 = f32[512]{0:T(512)S(1)} all-reduce(f32[512]{0:T(512)S(1)} %get-tuple-element.7), channel_id=1, replica_groups=mesh['section'=32,'tensor'=8] {'section','tensor'}, use_global_device_ids=true, to_apply=%region_3.4 | all-reduce | flops 512 | bytes 4096 | tf_op jit(solution)/shard_map/pmax | solution.py:19
  265.9 0.5 fusion
  266.4 74.4 %all-reduce.1 = (f32[512]{0:T(512)S(1)}, f32[512]{0:T(512)S(1)}) all-reduce(f32[512]{0:T(512)S(1)} %get-tuple-element.4, f32[512]{0:T(512)S(1)} %get-tuple-element.3), channel_id=1, replica_groups=mesh['section'=32,'tensor'=8] {'section','tensor'}, use_global_device_ids=true, to_apply=%region_8.9 | all-reduce | flops 1024 | bytes 8192 | tf_op jit(solution)/shard_map/psum | solution.py:21
  340.8 8.9 %fusion.6 = f32[512,4608]{1,0:T(8,128)} fusion(bf16[512,4608]{1,0:T(8,128)(2,1)} %reshape.132, f32[512,512]{0,1:T(8,128)S(1)} %get-tuple-element.8, f32[512]{0:T(512)S(1)} %get-tuple-element.6, s32[512]{0:T(512)S(1)} %copy-done, f32[512]{0:T(512)S(1)} %pmax.7, s32[512]{0:T(512)S(1)} %add.74, pred[512]{0:T(512)(128)(4,1)S(1)} %broadcast_in_dim.37), kind=kOutput, calls=%fused_computation.29 | convolution fusion | flops 2418278400 | bytes 15213056 | tf_op jit(solution)/shard_map/dot_general | solution.py:67
  349.7 0.6 dynamic_slice.15
  350.3 7.0 %convolution_convert_fusion.1 = bf16[512,4608]{1,0:T(8,128)(2,1)} fusion(bf16[512,4608]{1,0:T(8,128)(2,1)} %all-gather.2.cloned.1.call-done, f32[512,512]{0,1:T(8,128)S(1)} %get-tuple-element.8, f32[512]{0:T(512)S(1)} %get-tuple-element.6, s32[512]{0:T(512)S(1)} %copy-done, f32[512]{0:T(512)S(1)} %pmax.7, s32[512]{0:T(512)S(1)} %add.74, ...), kind=kOutput, calls=%fused_computation.1 | convolution fusion | flops 2420637696 | bytes 10494464 | tf_op jit(solution)/shard_map/dot_general | solution.py:71
  357.3 265.8 %all-reduce.4.cloned.1.call-done = f32[512,4608]{1,0:T(8,128)} async-done(((f32[512,4608]{1,0:T(8,128)}), f32[512,4608]{1,0:T(8,128)}) %all-reduce.4.cloned.1.call-update) | async-done | bytes 9437200
  623.1 1.5 constant_dynamic-slice_fusion
  (19 shorter events, 0.6 us)
Async XLA Ops:
  33.0 138.0 %all-to-all-start = ((bf16[32,2,36864]{2,1,0:T(2,128)(2,1)}), bf16[32,2,36864]{2,1,0:T(2,128)(2,1)}, u32[]{:S(2)}, u32[]{:S(2)}) async-start(bf16[32,2,36864]{2,1,0:T(2,128)(2,1)} %copy.10), calls=%async_computation | async-start | bytes 9437184 | tf_op jit(solution)/shard_map/all_to_all | solution.py:53
  45.0 134.4 %all-gather.2.cloned.1.call-start = ((), (), s32[]{:S(2)}) async-start(), calls=%async_computation.1 | async-start | bytes 4866048 | tf_op jit(solution)/shard_map/all_gather | solution.py:45
  45.8 577.3 %all-reduce.4.cloned.1.call-start = ((), (), s32[]{:S(2)}) async-start(), calls=%async_computation.2 | async-start | bytes 18874368
  179.4 86.5 %copy-start = (s32[512]{0:T(512)S(1)}, s32[512]{0:T(512)}, u32[]{:S(2)}) copy-start(s32[512]{0:T(512)} %param.7) | copy-start | bytes 6148
Sparse Core Ops, SparseCore 0:
  48.4 129.2 all-gather.1
  349.8 273.2 all-reduce.3
where the time goes:
time: 633 us; the launch traced here: 631 us
  waiting for transfers between devices  391 us (62%)
  blocking collectives  155 us (24%)
  local copies, waits for them, and re-layouts  28.6 us (5%)
  matrix products  27.9 us (4%)
  between operations  14.2 us (2%)
  starting transfers between devices  12.1 us (2%)
    unnamed x3, waiting for transfers between devices  266 us
    all_to_all x1, waiting for transfers between devices, on_device(): lax.all_to_all(packed, 'section', split_axis=0, concat_axis=0, tiled=True)  124 us
    pmax x1, blocking collectives, softmax_grad(): top = lax.pmax(jnp.max(masked, axis=1), ('section', 'tensor'))  80.3 us
    psum x1, blocking collectives, softmax_grad(): lax.psum((jnp.sum(shifted, axis=1), local_target), ('section', 'tensor'))  74.4 us
  transfers between devices with their start and end apart: 3, of which 2 were waited for; matrix products, arithmetic and copies ran while one was open for 3% of the time, Pallas kernels for 0%

commit v1 on v0

v1 whole, which is shorter than its diff:
```python
import jax
import jax.numpy as jnp
from jax import lax
from jax.sharding import PartitionSpec as P


def home_ranks(dest):
    count = dest.shape[1]
    same = dest[:, :, None] == dest[:, None, :]
    order = jnp.arange(count, dtype=jnp.int32)
    earlier = order[None, :] < order[:, None]
    return jnp.sum((same & earlier[None]).astype(jnp.int32), axis=2)


def on_device(hidden, head_weight, panel_section, targets):
    sections = lax.axis_size("section")
    tensors = lax.axis_size("tensor")
    myself = lax.axis_index("section")
    portion = lax.axis_index("tensor")
    per_section, rows, width = head_weight.shape
    slots = 5 * per_section // (4 * sections)
    panel_rows = rows * tensors
    dest = panel_section[:, 0].reshape(sections, per_section)
    my_dest = lax.dynamic_index_in_dim(dest, myself, 0, keepdims=True)
    my_rank = home_ranks(my_dest)[0]
    my_dest = my_dest[0]
    section_ids = jnp.arange(sections, dtype=jnp.int32)
    slot_ids = jnp.arange(slots, dtype=jnp.int32)
    send_map = (
        (my_dest[None, None, :] == section_ids[:, None, None])
        & (my_rank[None, None, :] == slot_ids[None, :, None])
    ).reshape(sections * slots, per_section)
    whole = lax.all_gather(hidden, "section", axis=0, tiled=True)
    tokens = whole.shape[0]
    weight = head_weight.reshape(per_section * rows, width)
    logits = lax.dot_general(
        weight, whole, (((1,), (1,)), ((), ())), preferred_element_type=jnp.float32
    )
    row = jnp.arange(per_section * rows, dtype=jnp.int32)
    row_ids = (myself * per_section + row // rows) * panel_rows + portion * rows + row % rows
    hits = row_ids[:, None] == targets[None, :]
    local_top = jnp.max(logits, axis=0)
    local_total = jnp.sum(jnp.exp(logits - local_top[None, :]), axis=0)
    local_picked = jnp.sum(jnp.where(hits, logits, 0.0), axis=0)
    top = lax.pmax(local_top, ("section", "tensor"))
    total, picked = lax.psum(
        (local_total * jnp.exp(local_top - top), local_picked), ("section", "tensor")
    )
    loss = jnp.log(total) + top - picked
    dlogits = (
        jnp.exp(logits - top[None, :]) / total[None, :] - hits.astype(jnp.float32)
    ).astype(jnp.bfloat16)
    packed = jnp.dot(
        send_map.astype(jnp.bfloat16),
        dlogits.reshape(per_section, rows * tokens),
        preferred_element_type=jnp.float32,
    ).astype(jnp.bfloat16)
    arrived = lax.all_to_all(
        packed.reshape(sections, slots * rows, tokens),
        "section",
        split_axis=0,
        concat_axis=0,
        tiled=True,
    )
    partial_grad = lax.dot_general(
        dlogits, weight, (((0,), (0,)), ((), ())), preferred_element_type=jnp.float32
    )
    hidden_grad = lax.psum_scatter(
        partial_grad, ("section", "tensor"), scatter_dimension=0, tiled=True
    )
    grads = lax.dot_general(
        arrived.reshape(sections * slots * rows, tokens),
        whole,
        (((1,), (0,)), ((), ())),
        preferred_element_type=jnp.float32,
    ).astype(jnp.bfloat16)
    slot_grads = grads.reshape(1, sections, slots, rows, width)
    own_rows = hidden.shape[0]
    own_loss = lax.dynamic_slice_in_dim(loss, myself * own_rows, own_rows)
    return (own_loss, hidden_grad, slot_grads)


def solution(mesh):
    in_specs = (P("section", None), P("section", "tensor", None), P(), P())
    out_specs = (
        P("section"),
        P(("section", "tensor"), None),
        P("section", None, None, "tensor", None),
    )
    return jax.shard_map(
        on_device, mesh=mesh, in_specs=in_specs, out_specs=out_specs, check_vma=False
    )
```

time: 633 us -> 552 us (0.87)
  waiting for transfers between devices: 391 us -> 353 us
  local copies, waits for them, and re-layouts: 28.6 us -> 4.19 us
  matrix products: 27.9 us -> 20.4 us
    all_to_all x1, waiting for transfers between devices: 124 us -> 18.1 us  [on_device(): lax.all_to_all(packed.reshape(sections, slots * rows, tokens), 'section',...]
    all_gather x1, waiting for transfers between devices: 0.01 us -> 87.2 us  [on_device(): whole = lax.all_gather(hidden, 'section', axis=0, tiled=True)]
    unnamed x3, waiting for transfers between devices: 266 us -> 248 us
    reshape x2, local copies, waits for them, and re-layouts: 16 us -> 1.28 us  [the longest x1 1.03 us: on_device(): packed.reshape(sections, slots * rows, tokens)]
    convert_element_type x1 -> x0, local copies, waits for them, and re-layouts: 9.38 us -> none  [on_device(): packed = jnp.einsum('dkj,jx->dkx', send_map, head_weight.reshape(per_sect...]
    dot_general x4, matrix products: 27.9 us -> 20.4 us  [the longest x1 7.44 us: on_device(): lax.dot_general(dlogits, weight, (((0,), (0,)), ((), ())), preferred_elem...]
  transfers between devices with their start and end apart: 3 -> 3, of which waited for: 2 -> 3; matrix products, arithmetic and copies ran while one was open for 3% -> 2% of each run, Pallas kernels for 0% -> 0%
where the time goes in v1:
time: 552 us; the launch traced here: 550 us
  waiting for transfers between devices  353 us (64%)
  blocking collectives  150 us (27%)
  matrix products  20.4 us (4%)
  between operations  14.1 us (3%)
  starting transfers between devices  6.51 us (1%)
    unnamed x3, waiting for transfers between devices  248 us
    all_gather x1, waiting for transfers between devices, on_device(): whole = lax.all_gather(hidden, 'section', axis=0, tiled=True)  87.2 us
    pmax x1, blocking collectives, on_device(): top = lax.pmax(local_top, ('section', 'tensor'))  77.8 us
    psum x1, blocking collectives, on_device(): lax.psum((local_total * jnp.exp(local_top - top), local_picked), ('sectio...  72.4 us
    all_to_all x1, waiting for transfers between devices, on_device(): lax.all_to_all(packed.reshape(sections, slots * rows, tokens), 'section',...  18.1 us
  transfers between devices with their start and end apart: 3, of which 3 were waited for; matrix products, arithmetic and copies ran while one was open for 2% of the time, Pallas kernels for 0%

profile of v1, /device:TPU:1, one launch (start us, length us, event | category | flops | bytes accessed | tf_op | source)
XLA Modules:
  0.0 550.3 jit_solution(4807874230371333246)
XLA Ops:
  7.2 0.0 all-gather.2.cloned.1.call-start
  7.2 0.7 all-gather.2.cloned.1.call-update
  7.9 0.0 all-reduce.4.cloned.1.call-start
  8.0 87.2 %all-gather.2.cloned.1.call-done = bf16[512,4608]{1,0:T(8,128)(2,1)} async-done(((bf16[16,4608]{1,0:T(8,128)(2,1)}), bf16[512,4608]{1,0:T(8,128)(2,1)}) %all-gather.2.cloned.1.call-update) | async-done | bytes 4718608 | tf_op jit(solution)/shard_map/all_gather | solution.py:33
  95.2 6.1 %fusion.19 = (f32[512]{0:T(512)S(1)}, f32[512,512]{1,0:T(8,128)S(1)}) fusion(bf16[512,4608]{1,0:T(8,128)(2,1)} %all-gather.2.cloned.1.call-done, bf16[64,8,4608]{2,1,0:T(8,128)(2,1)} %param.5), kind=kOutput, calls=%fused_computation.37 | convolution fusion | flops 2416180736 | bytes 10487808 | tf_op jit(solution)/shard_map/dot_general | solution.py:36
  101.2 77.8 %pmax.7 = f32[512]{0:T(512)S(1)} all-reduce(f32[512]{0:T(512)S(1)} %get-tuple-element.7), channel_id=1, replica_groups=mesh['section'=32,'tensor'=8] {'section','tensor'}, use_global_device_ids=true, to_apply=%region_2.3 | all-reduce | flops 512 | bytes 4096 | tf_op jit(solution)/shard_map/pmax | solution.py:45
  179.0 0.3 exponential_reduce_fusion
  179.3 72.4 %all-reduce.1 = (f32[512]{0:T(512)S(1)}, f32[512]{0:T(512)S(1)}) all-reduce(f32[512]{0:T(512)S(1)} %get-tuple-element.4, f32[512]{0:T(512)S(1)} %exponential_multiply_fusion), channel_id=1, replica_groups=mesh['section'=32,'tensor'=8] {'section','tensor'}, use_global_device_ids=true, to_apply=%region_5.6 | all-reduce | flops 1024 | bytes 8192 | tf_op jit(solution)/shard_map/psum | solution.py:46
  251.7 0.3 fusion.6
  252.0 7.4 %fusion = f32[512,4608]{1,0:T(8,128)} fusion(bf16[512,512]{1,0:T(8,128)(2,1)S(1)} %fusion.6, bf16[64,8,4608]{2,1,0:T(8,128)(2,1)} %param.5), kind=kOutput, calls=%fused_computation.1 | convolution fusion | flops 2415919104 | bytes 14680064 | tf_op jit(solution)/shard_map/dot_general | solution.py:65
  259.5 0.5 broadcast.155
  260.0 0.2 copy-done.1
  260.1 0.7 reduce.4
  260.8 0.1 reshape_squeeze.3
  260.9 0.2 convert_reduce_fusion
  261.2 0.2 reshape.193
  261.4 0.3 convolution_convert_fusion.1
  261.7 1.0 reshape.194
  262.7 6.4 %all-to-all-start = ((bf16[32,16,512]{2,1,0:T(8,128)(2,1)}), bf16[32,16,512]{2,1,0:T(8,128)(2,1)S(1)}, u32[]{:S(2)}, u32[]{:S(2)}) async-start(bf16[32,16,512]{2,1,0:T(8,128)(2,1)} %reshape.194), calls=%async_computation | async-start | bytes 1048576 | tf_op jit(solution)/shard_map/all_to_all | solution.py:58
  269.2 0.6 dynamic_slice.7
  269.8 18.1 %all-to-all-done = bf16[32,16,512]{2,1,0:T(8,128)(2,1)S(1)} async-done(((bf16[32,16,512]{2,1,0:T(8,128)(2,1)}), bf16[32,16,512]{2,1,0:T(8,128)(2,1)S(1)}, u32[]{:S(2)}, u32[]{:S(2)}) %all-to-all-start) | async-done | bytes 524320 | tf_op jit(solution)/shard_map/all_to_all | solution.py:58
  287.9 6.6 %convolution_convert_fusion = bf16[512,4608]{1,0:T(8,128)(2,1)} fusion(bf16[512,512]{1,0:T(8,128)(2,1)S(1)} %bitcast.18, bf16[512,4608]{1,0:T(8,128)(2,1)} %all-gather.2.cloned.1.call-done), kind=kOutput, calls=%fused_computation | convolution fusion | flops 2418278400 | bytes 9961472 | tf_op jit(solution)/shard_map/dot_general | solution.py:71
  294.5 247.5 %all-reduce.4.cloned.1.call-done = f32[512,4608]{1,0:T(8,128)} async-done(((f32[512,4608]{1,0:T(8,128)}), f32[512,4608]{1,0:T(8,128)}) %all-reduce.4.cloned.1.call-update) | async-done | bytes 9437200
  542.0 1.5 constant_dynamic-slice_fusion
  (12 shorter events, 0.1 us)
Async XLA Ops:
  7.2 88.0 %all-gather.2.cloned.1.call-start = ((), (), s32[]{:S(2)}) async-start(), calls=%async_computation.1 | async-start | bytes 4866048 | tf_op jit(solution)/shard_map/all_gather | solution.py:33
  7.9 534.1 %all-reduce.4.cloned.1.call-start = ((), (), s32[]{:S(2)}) async-start(), calls=%async_computation.2 | async-start | bytes 18874368
  8.0 171.1 %copy-start = (s32[512]{0:T(512)S(1)}, s32[512]{0:T(512)}, u32[]{:S(2)}) copy-start(s32[512]{0:T(512)} %param.7) | copy-start | bytes 6148
  259.4 0.7 copy-start.1
  262.7 25.1 %all-to-all-start = ((bf16[32,16,512]{2,1,0:T(8,128)(2,1)}), bf16[32,16,512]{2,1,0:T(8,128)(2,1)S(1)}, u32[]{:S(2)}, u32[]{:S(2)}) async-start(bf16[32,16,512]{2,1,0:T(8,128)(2,1)} %reshape.194), calls=%async_computation | async-start | bytes 1048576 | tf_op jit(solution)/shard_map/all_to_all | solution.py:58
Sparse Core Ops, SparseCore 0:
  10.6 84.5 all-gather.1
  259.6 282.3 all-reduce.3

commit v2 on v0

v2 whole, which is shorter than its diff:
```python
import functools

import jax
import jax.numpy as jnp
from jax import lax
from jax.experimental import pallas as pl
from jax.experimental.pallas import tpu as pltpu
from jax.sharding import PartitionSpec as P

MESH = pl.DeviceIdType.MESH
NZ, NX, NY, NC = 8, 4, 4, 2
NS, NT = NZ * NX, NY * NC
D = 4608
TOK = 512
ROWS = 16
VOC = 512
QUART = D // 4
WIDE = 768
NARROW = 384
DX = (1, 3, 2)
NT_DIMS = (((1,), (1,)), ((), ()))


def mod(a, n):
    return lax.rem(a + 2 * n, n)


def body(
    hidden_ref,
    weight_hbm,
    panels_ref,
    targets_ref,
    loss_ref,
    hgrad_ref,
    slots_hbm,
    w,
    hb,
    lbuf,
    dlb,
    pack,
    tcol,
    a2as,
    a2ar,
    st_s,
    st_z,
    st_x,
    st_t,
    r0s,
    r0r,
    own,
    ys,
    yr,
    xs,
    xr,
    x2s,
    x2r,
    acc2,
    y2s,
    y2r,
    zf,
    zs,
    zr,
    fin_s,
    fin_r,
    stage,
    local_sem,
    out_sem,
    gz0,
    gx0,
    gx1,
    gz1,
    gcore,
    bsem,
    asem,
    r0sem,
    ysem,
    xsem,
    x2sem,
    y2sem,
    zsem,
    fsem,
):
    sec = lax.axis_index("section")
    ten = lax.axis_index("tensor")
    z, x = sec // NX, sec % NX
    y, c = ten // NC, ten % NC
    sgn = 1 - 2 * c
    q0, q1 = 2 * c, 2 * c + 1

    def at_z(zz):
        return (zz * NX + x, ten)

    def at_x(xx):
        return (z * NX + xx, ten)

    def at_y(yy):
        return (sec, yy * NC + c)

    other = (sec, y * NC + 1 - c)
    sent = []

    def push(src, dst, sems, where, dev):
        copy = pltpu.make_async_remote_copy(
            src_ref=src,
            dst_ref=dst,
            send_sem=sems.at[(0, *where)],
            recv_sem=sems.at[(1, *where)],
            device_id=dev,
            device_id_type=MESH,
        )
        copy.start()
        sent.append(copy)

    def landed(dst, sems, where):
        pltpu.make_async_copy(dst, dst, sems.at[(1, *where)]).wait()

    w_in = pltpu.make_async_copy(weight_hbm, w, local_sem.at[0])
    w_in.start()
    for part in range(2):
        for core in range(2):
            @pl.when(c == core)
            def _():
                lo = (2 * core + part) * QUART
                hb[2 * core + part, z, x] = hidden_ref[:, lo:lo + QUART]

    barrier = pltpu.get_barrier_semaphore()

    def greet_sections(i, carry):
        pl.semaphore_signal(
            barrier, inc=1, device_id=(mod(sec + i, NS), ten), device_id_type=MESH
        )
        return carry

    lax.fori_loop(1, NS, greet_sections, 0)

    def greet_tensors(i, carry):
        pl.semaphore_signal(
            barrier, inc=1, device_id=(sec, mod(ten + i, NT)), device_id_type=MESH
        )
        return carry

    lax.fori_loop(1, NT, greet_tensors, 0)
    pl.semaphore_wait(barrier, NS - 1 + NT - 1)

    fwd, bwd = at_z(mod(z + sgn, NZ)), at_z(mod(z - sgn, NZ))

    def back(k):
        return mod(z - k * sgn, NZ)

    def ahead(k):
        return mod(z + k * sgn, NZ)

    def send_z(q, sems, zz, xx, way, k, *stream):
        piece = hb.at[q, zz, xx]
        push(piece, piece, sems, (way, k, *stream), fwd if way == 0 else bwd)

    def send_x(q, sems, zz, *where):
        for i, dx in enumerate(DX):
            piece = hb.at[q, zz, x]
            push(piece, piece, sems, (i, *where), at_x(mod(x + dx, NX)))

    streams = [x] + [mod(x - dx, NX) for dx in DX]

    send_z(q0, gz0, z, x, 0, 0)
    send_z(q0, gz0, z, x, 1, 0)
    send_x(q1, gx1, z)
    send_z(q1, gz1, z, x, 0, 0, 0)
    send_z(q1, gz1, z, x, 1, 0, 0)
    send_x(q0, gx0, z, 0)

    w_in.wait()
    lane = lax.broadcasted_iota(jnp.int32, (VOC, VOC), 1)
    row = lax.broadcasted_iota(jnp.int32, (VOC, VOC), 0)
    base = pl.multiple_of((sec // 2) * 128, 128)
    names = panels_ref[:, pl.ds(base, 128)].astype(jnp.float32)
    names = jnp.broadcast_to(names, (8, 128)).astype(jnp.bfloat16)
    spread = (
        lax.broadcasted_iota(jnp.int32, (128, VOC), 0)
        == lax.broadcasted_iota(jnp.int32, (128, VOC), 1) // 8 + (sec % 2) * 64
    )
    named = jnp.dot(
        names, spread.astype(jnp.float32).astype(jnp.bfloat16),
        preferred_element_type=jnp.float32,
    )[:1]
    named_col = jnp.transpose(jnp.broadcast_to(named, (128, VOC)))[:, :1]
    earlier = (named_col == named) & (row // 8 < lane // 8)
    rank = jnp.sum(jnp.where(earlier, 0.125, 0.0), axis=0, keepdims=True)
    wanted = (row // 16).astype(jnp.float32)
    place = (row // 8 % 2).astype(jnp.float32)
    chosen = (wanted == named) & (place == rank) & (row % 8 == lane % 8)
    pack[...] = jnp.where(chosen, 1.0, 0.0).astype(jnp.bfloat16)
    ids = jnp.broadcast_to(targets_ref[...].astype(jnp.float32), (128, TOK))
    tcol[...] = jnp.transpose(ids)

    def step0(k):
        landed(hb.at[q0, back(k + 1), x], gz0, (0, k))
        if k < 3:
            send_z(q0, gz0, back(k + 1), x, 0, k + 1)
        send_x(q0, gx0, back(k + 1), 2 * k + 1)
        if k < 3:
            landed(hb.at[q0, ahead(k + 1), x], gz0, (1, k))
            if k < 2:
                send_z(q0, gz0, ahead(k + 1), x, 1, k + 1)
            send_x(q0, gx0, ahead(k + 1), 2 * k + 2)

    def start1():
        for i in range(3):
            landed(hb.at[q1, z, streams[i + 1]], gx1, (i,))
            send_z(q1, gz1, z, streams[i + 1], 0, 0, i + 1)
            send_z(q1, gz1, z, streams[i + 1], 1, 0, i + 1)
        cross(q1, z, 1, 0)

    def step1(k):
        for i, xx in enumerate(streams):
            landed(hb.at[q1, back(k + 1), xx], gz1, (0, k, i))
            if k < 3:
                send_z(q1, gz1, back(k + 1), xx, 0, k + 1, i)
            if k < 3:
                landed(hb.at[q1, ahead(k + 1), xx], gz1, (1, k, i))
                if k < 2:
                    send_z(q1, gz1, ahead(k + 1), xx, 1, k + 1, i)
        cross(q1, back(k + 1), 1, 2 * k + 1)
        if k < 3:
            cross(q1, ahead(k + 1), 1, 2 * k + 2)

    def cross(q, zz, part, n):
        piece = hb.at[q, zz]
        push(piece, piece, gcore, (part, n), other)

    order = [z]
    for k in range(4):
        order.append(back(k + 1))
        if k < 3:
            order.append(ahead(k + 1))

    def finish0(n):
        for i in range(3):
            landed(hb.at[q0, order[n], streams[i + 1]], gx0, (i, n))
        cross(q0, order[n], 0, n)

    step0(0)
    start1()
    step0(1)
    step1(0)
    step0(2)
    step0(3)
    finish0(0)
    finish0(1)
    finish0(2)
    step1(1)
    finish0(3)
    finish0(4)
    step1(2)
    finish0(5)
    finish0(6)
    step1(3)
    finish0(7)

    def logits(first, last):
        for n in range(first, last):
            mirror = n if n in (0, 7) else (n + 1 if n % 2 else n - 1)
            for part in range(2):
                landed(hb.at[2 - 2 * c + part, order[n]], gcore, (part, mirror))
        count = last - first
        left = jnp.concatenate(
            [
                jnp.concatenate(
                    [hb[q, order[n]].reshape(64, QUART) for n in range(first, last)],
                    axis=0,
                )
                for q in range(4)
            ],
            axis=1,
        )
        product = lax.dot_general(
            left, w[...], NT_DIMS, preferred_element_type=jnp.float32
        )
        for i in range(count):
            lbuf[order[first + i]] = product[i * 64:(i + 1) * 64]

    logits(0, 5)
    logits(5, 8)

    scores = lbuf[...].reshape(TOK, VOC)
    lane1 = lax.broadcasted_iota(jnp.int32, (1, VOC), 1)
    ids_row = (
        (sec * 64 + lane1 // 8) * 64 + ten * 8 + lane1 % 8
    ).astype(jnp.float32)
    hits = tcol[:, :1] == ids_row
    top1 = jnp.max(scores, axis=1, keepdims=True)
    total1 = jnp.sum(jnp.exp(scores - top1), axis=1, keepdims=True)
    picked1 = jnp.sum(jnp.where(hits, scores, 0.0), axis=1, keepdims=True)
    lanes = lax.broadcasted_iota(jnp.int32, (TOK, 128), 1)
    stats = jnp.where(lanes == 0, top1, jnp.where(lanes == 1, total1, picked1))
    st_s[0] = jnp.transpose(stats)[:8]

    def merge(mine, parts):
        tops = [mine[0:1]] + [p[0:1] for p in parts]
        best = functools.reduce(jnp.maximum, tops)
        total = mine[1:2] * jnp.exp(mine[0:1] - best)
        picked = mine[2:3]
        for p in parts:
            total += p[1:2] * jnp.exp(p[0:1] - best)
            picked += p[2:3]
        return best, total, picked

    def rows8(best, total, picked):
        sub = lax.broadcasted_iota(jnp.int32, (8, TOK), 0)
        return jnp.where(sub == 0, best, jnp.where(sub == 1, total, picked))

    for dz in range(1, NZ):
        push(st_s.at[0], st_z.at[dz - 1], bsem, (0, dz - 1), at_z(mod(z + dz, NZ)))
    for dz in range(1, NZ):
        landed(st_z.at[dz - 1], bsem, (0, dz - 1))
    st_s[1] = rows8(*merge(st_s[0], [st_z[i] for i in range(NZ - 1)]))
    for dx in range(1, NX):
        push(st_s.at[1], st_x.at[dx - 1], bsem, (1, dx - 1), at_x(mod(x + dx, NX)))
    for dx in range(1, NX):
        landed(st_x.at[dx - 1], bsem, (1, dx - 1))
    st_s[2] = rows8(*merge(st_s[1], [st_x[i] for i in range(NX - 1)]))
    for dt in range(1, NT):
        push(st_s.at[2], st_t.at[dt - 1], bsem, (2, dt - 1), (sec, mod(ten + dt, NT)))
    for dt in range(1, NT):
        landed(st_t.at[dt - 1], bsem, (2, dt - 1))
    best, total, picked = merge(st_s[2], [st_t[i] for i in range(NT - 1)])
    loss_ref[...] = jnp.log(total) + best - picked
    back_cols = jnp.transpose(
        jnp.concatenate(
            [rows8(best, 1.0 / total, picked), jnp.zeros((120, TOK), jnp.float32)], axis=0
        )
    )
    dl = jnp.exp(scores - back_cols[:, :1]) * back_cols[:, 1:2]
    dlb[...] = (dl - jnp.where(hits, 1.0, 0.0)).astype(jnp.bfloat16)

    half = TOK // 2
    theirs = pl.multiple_of((1 - c) * half, half)
    ours = pl.multiple_of(c * half, half)

    def y_cols(yy):
        return pl.multiple_of(yy * WIDE, WIDE)

    chunks = [
        ("y", mod(y + 2, NY)),
        ("x", 0),
        ("y", mod(y + 1, NY)),
        ("x", 1),
        ("y", mod(y + 3, NY)),
        ("y", y),
    ]
    y_slot = {0: 0, 2: 1, 4: 2}
    x_at = (1, 3)

    def compute(p):
        kind, i = chunks[p]
        lo = y_cols(i) if kind == "y" else NY * WIDE + i * WIDE
        cols = w[:, pl.ds(lo, WIDE)]
        give = jnp.dot(dlb[pl.ds(theirs, half), :], cols, preferred_element_type=jnp.float32)
        r0s[p] = give.astype(jnp.bfloat16).reshape(4, NX, ROWS, WIDE)
        push(r0s.at[p], r0r.at[p], r0sem, (p,), other)
        keep = jnp.dot(dlb[pl.ds(ours, half), :], cols, preferred_element_type=jnp.float32)
        own[p] = keep.reshape(4, NX, ROWS, WIDE)

    def pass_on(p):
        kind, i = chunks[p]
        landed(r0r.at[p], r0sem, (p,))
        both = own[p] + r0r[p].astype(jnp.float32)
        if kind == "x":
            own[p] = both
            xs[i] = both.astype(jnp.bfloat16)
            for n, dx in enumerate(DX):
                push(
                    xs.at[i, :, mod(x + dx, NX)], xr.at[i, n], xsem, (i, n),
                    at_x(mod(x + dx, NX)),
                )
        elif p == 5:
            own[p] = both
        else:
            n = y_slot[p]
            ys[n] = both.astype(jnp.bfloat16)
            push(ys.at[n], yr.at[n], ysem, (n,), at_y(i))

    compute(0)
    compute(1)
    pass_on(0)
    packed = lax.dot_general(
        pack[...], dlb[...], NT_DIMS, preferred_element_type=jnp.float32
    )
    a2as[...] = packed.astype(jnp.bfloat16).reshape(NS, ROWS, TOK)

    def scatter(i, carry):
        to = mod(sec + i, NS)
        pltpu.make_async_remote_copy(
            src_ref=a2as.at[to],
            dst_ref=a2ar.at[sec],
            send_sem=asem.at[0],
            recv_sem=asem.at[1],
            device_id=(to, ten),
            device_id_type=MESH,
        ).start()
        return carry

    lax.fori_loop(1, NS, scatter, 0)
    compute(2)
    pass_on(1)
    compute(3)
    pass_on(2)
    compute(4)
    pass_on(3)
    compute(5)
    pass_on(4)
    pass_on(5)

    for j in range(2):
        for n in range(3):
            landed(xr.at[j, n], xsem, (j, n))
        got = own[x_at[j], :, x]
        for n in range(3):
            got += xr[j, n].astype(jnp.float32)
        for h in range(2):
            piece = got[:, :, h * NARROW:(h + 1) * NARROW]
            acc2[2 * j + h] = piece
            y2s[2 * j + h] = piece.astype(jnp.bfloat16)
    for n in range(3):
        to = mod(y + n + 1, NY)
        push(y2s.at[to], y2r.at[n], y2sem, (n,), at_y(to))

    a2ar[sec] = a2as[sec]
    pltpu.make_async_copy(
        a2ar.at[pl.ds(0, NS - 1)], a2ar.at[pl.ds(0, NS - 1)], asem.at[1]
    ).wait()
    outs = []
    for q in range(4):
        if q >= 2:
            outs[q - 2].wait()
        grads = jnp.dot(
            a2ar[...].reshape(NS * ROWS, TOK),
            hb[q].reshape(TOK, QUART),
            preferred_element_type=jnp.float32,
        )
        stage[q % 2] = grads.astype(jnp.bfloat16)
        out = pltpu.make_async_copy(
            stage.at[q % 2], slots_hbm.at[:, q * QUART:(q + 1) * QUART], out_sem.at[q]
        )
        out.start()
        outs.append(out)

    for n in range(3):
        landed(yr.at[n], ysem, (n,))
    both = own[5]
    for n in range(3):
        both += yr[n].astype(jnp.float32)
    own[5] = both
    x2s[...] = both.astype(jnp.bfloat16)
    for n, dx in enumerate(DX):
        to = mod(x + dx, NX)
        push(x2s.at[:, to], x2r.at[n], x2sem, (n,), at_x(to))

    for n in range(3):
        landed(y2r.at[n], y2sem, (n,))
    narrow = acc2[y]
    for n in range(3):
        narrow += y2r[n].astype(jnp.float32)
    for n in range(3):
        landed(x2r.at[n], x2sem, (n,))
    wide = own[5, :, x]
    for n in range(3):
        wide += x2r[n].astype(jnp.float32)
    zf[:, :, :WIDE] = wide
    zf[:, :, WIDE:] = narrow
    zs[:, :, :WIDE] = wide.astype(jnp.bfloat16)
    zs[:, :, WIDE:] = narrow.astype(jnp.bfloat16)
    mine = z // 4 == c
    z_copies = []
    for i in range(4):
        to = 4 * c + i
        copy = pltpu.make_async_remote_copy(
            src_ref=zs.at[i],
            dst_ref=zr.at[mod(to - z, NZ)],
            send_sem=zsem.at[0, i],
            recv_sem=zsem.at[1, 0],
            device_id=at_z(to),
            device_id_type=MESH,
        )
        z_copies.append((to, copy))

        @pl.when(to != z)
        def _():
            copy.start()

    f_copies = []
    for t in range(NT):
        copy = pltpu.make_async_remote_copy(
            src_ref=fin_s.at[t],
            dst_ref=fin_r.at[y],
            send_sem=fsem.at[0, t],
            recv_sem=fsem.at[1, y],
            device_id=(sec, jnp.int32(t)),
            device_id_type=MESH,
        )
        f_copies.append(copy)

    @pl.when(mine)
    def _():
        zr[0] = jnp.zeros((ROWS, QUART), jnp.bfloat16)
        pltpu.make_async_copy(
            zr.at[pl.ds(1, NZ - 1)], zr.at[pl.ds(1, NZ - 1)], zsem.at[1, 0]
        ).wait()
        final = zf[z % 4]
        for i in range(1, NZ):
            final += zr[i].astype(jnp.float32)
        for t in range(NT):
            fin_s[t] = final[2 * t:2 * t + 2]
        for t in range(NT):
            @pl.when(ten != t)
            def _():
                f_copies[t].start()

        fin_r[y] = fin_s[ten]

    for i in range(NY):
        @pl.when(jnp.logical_not(mine & (y == i)))
        def _():
            landed(fin_r.at[i], fsem, (i,))

        hgrad_ref[:, i * WIDE:(i + 1) * WIDE] = fin_r[i, :, :WIDE]
        hgrad_ref[:, NY * WIDE + i * NARROW:NY * WIDE + (i + 1) * NARROW] = fin_r[
            i, :, WIDE:
        ]

    @pl.when(mine)
    def _():
        for t in range(NT):
            @pl.when(ten != t)
            def _():
                f_copies[t].wait_send()

    for to, copy in z_copies:
        @pl.when(to != z)
        def _():
            copy.wait_send()

    for copy in sent:
        copy.wait_send()
    pltpu.make_async_copy(
        a2as.at[pl.ds(0, NS - 1)], a2as.at[pl.ds(0, NS - 1)], asem.at[0]
    ).wait()
    outs[2].wait()
    outs[3].wait()


def on_device(hidden, head_weight, panel_section, targets):
    per_section, rows, width = head_weight.shape
    bf16, f32 = jnp.bfloat16, jnp.float32
    vmem = pl.BlockSpec(memory_space=pltpu.VMEM)
    hbm = pl.BlockSpec(memory_space=pl.ANY)
    dma = pltpu.SemaphoreType.DMA
    loss, hidden_grad, grads = pl.pallas_call(
        body,
        name="head_step",
        out_shape=(
            jax.ShapeDtypeStruct((1, TOK), f32),
            jax.ShapeDtypeStruct((2, D), f32),
            jax.ShapeDtypeStruct((NS * ROWS, D), bf16),
        ),
        in_specs=[vmem, hbm, vmem, vmem],
        out_specs=(vmem, vmem, hbm),
        scratch_shapes=[
            pltpu.VMEM((VOC, D), bf16),
            pltpu.VMEM((4, NZ, NX, ROWS, QUART), bf16),
            pltpu.VMEM((NZ, 64, VOC), f32),
            pltpu.VMEM((TOK, VOC), bf16),
            pltpu.VMEM((VOC, VOC), bf16),
            pltpu.VMEM((TOK, 128), f32),
            pltpu.VMEM((NS, ROWS, TOK), bf16),
            pltpu.VMEM((NS, ROWS, TOK), bf16),
            pltpu.VMEM((3, 8, TOK), f32),
            pltpu.VMEM((NZ - 1, 8, TOK), f32),
            pltpu.VMEM((NX - 1, 8, TOK), f32),
            pltpu.VMEM((NT - 1, 8, TOK), f32),
            pltpu.VMEM((6, 4, NX, ROWS, WIDE), bf16),
            pltpu.VMEM((6, 4, NX, ROWS, WIDE), bf16),
            pltpu.VMEM((6, 4, NX, ROWS, WIDE), f32),
            pltpu.VMEM((3, 4, NX, ROWS, WIDE), bf16),
            pltpu.VMEM((3, 4, NX, ROWS, WIDE), bf16),
            pltpu.VMEM((2, 4, NX, ROWS, WIDE), bf16),
            pltpu.VMEM((2, 3, 4, ROWS, WIDE), bf16),
            pltpu.VMEM((4, NX, ROWS, WIDE), bf16),
            pltpu.VMEM((3, 4, ROWS, WIDE), bf16),
            pltpu.VMEM((4, 4, ROWS, NARROW), f32),
            pltpu.VMEM((4, 4, ROWS, NARROW), bf16),
            pltpu.VMEM((3, 4, ROWS, NARROW), bf16),
            pltpu.VMEM((4, ROWS, QUART), f32),
            pltpu.VMEM((4, ROWS, QUART), bf16),
            pltpu.VMEM((NZ, ROWS, QUART), bf16),
            pltpu.VMEM((NT, 2, QUART), f32),
            pltpu.VMEM((NY, 2, QUART), f32),
            pltpu.VMEM((2, NS * ROWS, QUART), bf16),
            dma((1,)),
            dma((4,)),
            dma((2, 2, 4)),
            dma((2, 3, 8)),
            dma((2, 3)),
            dma((2, 2, 4, 4)),
            dma((2, 2, 8)),
            dma((2, 3, 7)),
            dma((2,)),
            dma((2, 6)),
            dma((2, 3)),
            dma((2, 2, 3)),
            dma((2, 3)),
            dma((2, 3)),
            dma((2, 4)),
            dma((2, 8)),
        ],
        compiler_params=pltpu.CompilerParams(
            collective_id=0, has_side_effects=True, vmem_limit_bytes=60 * 2**20
        ),
    )(
        hidden,
        head_weight.reshape(per_section * rows, width),
        panel_section.reshape(1, -1),
        targets.reshape(1, -1),
    )
    own_rows = hidden.shape[0]
    myself = lax.axis_index("section")
    own_loss = lax.dynamic_slice_in_dim(loss[0], myself * own_rows, own_rows)
    return (own_loss, hidden_grad, grads.reshape(1, NS, 2, rows, width))


def solution(mesh):
    in_specs = (P("section", None), P("section", "tensor", None), P(), P())
    out_specs = (
        P("section"),
        P(("section", "tensor"), None),
        P("section", None, None, "tensor", None),
    )
    return jax.shard_map(
        on_device, mesh=mesh, in_specs=in_specs, out_specs=out_specs, check_vma=False
    )
```

time: 633 us -> 103 us (0.16)
  waiting for transfers between devices: 391 us -> 0 us
  blocking collectives: 155 us -> 0 us
  Pallas kernels: 0 us -> 94.9 us
  matrix products: 27.9 us -> 0 us
  local copies, waits for them, and re-layouts: 28.6 us -> 7.45 us
  between operations: 14.2 us -> 0.65 us
  starting transfers between devices: 12.1 us -> 0 us
    unnamed x3 -> x0, waiting for transfers between devices: 266 us -> none
    all_to_all x1 -> x0, waiting for transfers between devices: 124 us -> none  [on_device(): lax.all_to_all(packed, 'section', split_axis=0, concat_axis=0, tiled=True)]
    pallas_call x0 -> x1, Pallas kernels: none -> 94.9 us  [on_device(): pl.pallas_call(body, name='head_step', out_shape=(jax.ShapeDtypeStruct((1...]
    pmax x1 -> x0, blocking collectives: 80.3 us -> none  [softmax_grad(): top = lax.pmax(jnp.max(masked, axis=1), ('section', 'tensor'))]
    psum x1 -> x0, blocking collectives: 74.4 us -> none  [softmax_grad(): lax.psum((jnp.sum(shifted, axis=1), local_target), ('section', 'tensor'))]
    dot_general x4 -> x0, matrix products: 27.9 us -> none  [the longest x1 8.85 us: on_device(): partial_grad = jnp.dot(dlogits, panels, preferred_element_type=jnp.float32)]
    reshape x2 -> x0, local copies, waits for them, and re-layouts: 16 us -> none  [the longest x1 8.3 us: on_device(): panels = arrived.reshape(sections * slots * rows, width)]
    all_to_all x1 -> x0, starting transfers between devices: 12 us -> none  [on_device(): lax.all_to_all(packed, 'section', split_axis=0, concat_axis=0, tiled=True)]
  transfers between devices with their start and end apart: 3 -> 0, of which waited for: 2 -> 0; matrix products, arithmetic and copies ran while one was open for 3% -> 0% of each run, Pallas kernels for 0% -> 0%
where the time goes in v2:
time: 103 us
  Pallas kernels  94.9 us (92%)
  local copies, waits for them, and re-layouts  7.45 us (7%)
    pallas_call x1, Pallas kernels, on_device(): pl.pallas_call(body, name='head_step', out_shape=(jax.ShapeDtypeStruct((1...  94.9 us
    unnamed x2, local copies, waits for them, and re-layouts  6.21 us

profile of v2, /device:TPU:1, one launch (start us, length us, event | category | flops | bytes accessed | tf_op | source)
XLA Modules:
  0.0 103.0 jit_solution(11813457585518382791)
XLA Ops:
  0.6 94.9 %head_step.1 = (f32[1,512]{1,0:T(1,128)}, f32[2,4608]{1,0:T(2,128)}, bf16[512,4608]{1,0:T(8,128)(2,1)}) custom-call(bf16[16,4608]{1,0:T(8,128)(2,1)} %hidden_ref.1, bf16[512,4608]{1,0:T(8,128)(2,1)} %bitcast.6, s32[1,2048]{1,0:T(1,128)} %bitcast.8, s32[1,512]{1,0:T(1,128)} %bitcast.9), custom_call_target="tpu_custom_call" | custom-call | tf_op jit(solution)/shard_map/head_step/pallas_call | solution.py:557
  95.6 1.2 %dynamic-slice_bitcast_fusion = f32[16]{0:T(128)} fusion(f32[1,512]{1,0:T(1,128)} %get-tuple-element.6, s32[]{:T(128)S(6)} %select_n.3), kind=kLoop, calls=%fused_computation | loop fusion | bytes 132 | tf_op jit(solution)/shard_map/dynamic_slice | solution.py:626
  96.8 1.4 %copy.9 = f32[2,4608]{1,0:T(2,128)} copy(f32[2,4608]{1,0:T(2,128)} %get-tuple-element.13) | data formatting | bytes 73728
  98.2 4.8 %copy.10 = bf16[1,32,2,8,4608]{4,3,2,1,0:T(8,128)(2,1)} copy(bf16[1,32,2,8,4608]{4,3,2,1,0:T(8,128)(2,1)} %bitcast.7) | data formatting | bytes 9437184

commit v3 on v2

--- a/solution.py
+++ b/solution.py
@@ -18,6 +18,7 @@
 WIDE = 768
 NARROW = 384
 DX = (1, 3, 2)
+ROUNDS = (2, 1, 3, 0)
 NT_DIMS = (((1,), (1,)), ((), ()))
 
 
@@ -32,7 +33,7 @@
     targets_ref,
     loss_ref,
     hgrad_ref,
-    slots_hbm,
+    slots_ref,
     w,
     hb,
     lbuf,
@@ -58,13 +59,13 @@
     y2s,
     y2r,
     zf,
-    zs,
-    zr,
+    zsw,
+    zsn,
+    zrw,
+    zrn,
     fin_s,
     fin_r,
-    stage,
     local_sem,
-    out_sem,
     gz0,
     gx0,
     gx1,
@@ -210,8 +211,9 @@
             send_z(q1, gz1, z, streams[i + 1], 1, 0, i + 1)
         cross(q1, z, 1, 0)
 
-    def step1(k):
-        for i, xx in enumerate(streams):
+    def step1(k, first, last):
+        for i in range(first, last):
+            xx = streams[i]
             landed(hb.at[q1, back(k + 1), xx], gz1, (0, k, i))
             if k < 3:
                 send_z(q1, gz1, back(k + 1), xx, 0, k + 1, i)
@@ -219,9 +221,10 @@
                 landed(hb.at[q1, ahead(k + 1), xx], gz1, (1, k, i))
                 if k < 2:
                     send_z(q1, gz1, ahead(k + 1), xx, 1, k + 1, i)
-        cross(q1, back(k + 1), 1, 2 * k + 1)
-        if k < 3:
-            cross(q1, ahead(k + 1), 1, 2 * k + 2)
+        if last == 4:
+            cross(q1, back(k + 1), 1, 2 * k + 1)
+            if k < 3:
+                cross(q1, ahead(k + 1), 1, 2 * k + 2)
 
     def cross(q, zz, part, n):
         piece = hb.at[q, zz]
@@ -240,20 +243,23 @@
 
     step0(0)
     start1()
+    step1(0, 0, 1)
     step0(1)
-    step1(0)
+    step1(0, 1, 4)
+    finish0(0)
+    step1(1, 0, 1)
     step0(2)
-    step0(3)
-    finish0(0)
+    step1(1, 1, 4)
     finish0(1)
     finish0(2)
-    step1(1)
+    step1(2, 0, 1)
+    step0(3)
+    step1(2, 1, 4)
     finish0(3)
     finish0(4)
-    step1(2)
+    step1(3, 0, 4)
     finish0(5)
     finish0(6)
-    step1(3)
     finish0(7)
 
     def logits(first, last):
@@ -292,38 +298,41 @@
     picked1 = jnp.sum(jnp.where(hits, scores, 0.0), axis=1, keepdims=True)
     lanes = lax.broadcasted_iota(jnp.int32, (TOK, 128), 1)
     stats = jnp.where(lanes == 0, top1, jnp.where(lanes == 1, total1, picked1))
-    st_s[0] = jnp.transpose(stats)[:8]
+    stats = jnp.transpose(stats)
+    mine3 = (stats[0:1], stats[1:2], stats[2:3])
+
+    def triple(ref, i):
+        return tuple(ref[i, :, n * TOK:(n + 1) * TOK] for n in range(3))
 
     def merge(mine, parts):
-        tops = [mine[0:1]] + [p[0:1] for p in parts]
-        best = functools.reduce(jnp.maximum, tops)
-        total = mine[1:2] * jnp.exp(mine[0:1] - best)
-        picked = mine[2:3]
+        best = functools.reduce(jnp.maximum, [p[0] for p in parts], mine[0])
+        total = mine[1] * jnp.exp(mine[0] - best)
+        picked = mine[2]
         for p in parts:
-            total += p[1:2] * jnp.exp(p[0:1] - best)
-            picked += p[2:3]
+            total += p[1] * jnp.exp(p[0] - best)
+            picked += p[2]
         return best, total, picked
+
+    def share(mine, phase, got, count, device):
+        for n in range(3):
+            st_s[phase, :, n * TOK:(n + 1) * TOK] = mine[n]
+        for i in range(1, count):
+            push(st_s.at[phase], got.at[i - 1], bsem, (phase, i - 1), device(i))
+        for i in range(1, count):
+            landed(got.at[i - 1], bsem, (phase, i - 1))
+        return merge(mine, [triple(got, i) for i in range(count - 1)])
 
     def rows8(best, total, picked):
         sub = lax.broadcasted_iota(jnp.int32, (8, TOK), 0)
         return jnp.where(sub == 0, best, jnp.where(sub == 1, total, picked))
 
-    for dz in range(1, NZ):
-        push(st_s.at[0], st_z.at[dz - 1], bsem, (0, dz - 1), at_z(mod(z + dz, NZ)))
-    for dz in range(1, NZ):
-        landed(st_z.at[dz - 1], bsem, (0, dz - 1))
-    st_s[1] = rows8(*merge(st_s[0], [st_z[i] for i in range(NZ - 1)]))
-    for dx in range(1, NX):
-        push(st_s.at[1], st_x.at[dx - 1], bsem, (1, dx - 1), at_x(mod(x + dx, NX)))
-    for dx in range(1, NX):
-        landed(st_x.at[dx - 1], bsem, (1, dx - 1))
-    st_s[2] = rows8(*merge(st_s[1], [st_x[i] for i in range(NX - 1)]))
-    for dt in range(1, NT):
-        push(st_s.at[2], st_t.at[dt - 1], bsem, (2, dt - 1), (sec, mod(ten + dt, NT)))
-    for dt in range(1, NT):
-        landed(st_t.at[dt - 1], bsem, (2, dt - 1))
-    best, total, picked = merge(st_s[2], [st_t[i] for i in range(NT - 1)])
-    loss_ref[...] = jnp.log(total) + best - picked
+    mine3 = share(mine3, 0, st_z, NZ, lambda i: at_z(mod(z + i, NZ)))
+    mine3 = share(mine3, 1, st_x, NX, lambda i: at_x(mod(x + i, NX)))
+    best, total, picked = share(
+        mine3, 2, st_t, NT, lambda i: (sec, mod(ten + i, NT))
+    )
+    loss = jnp.broadcast_to(jnp.log(total) + best - picked, (8, TOK))
+    loss_ref[...] = pltpu.roll(loss, TOK - sec * ROWS, 1)[:1, :ROWS]
     back_cols = jnp.transpose(
         jnp.concatenate(
             [rows8(best, 1.0 / total, picked), jnp.zeros((120, TOK), jnp.float32)], axis=0
@@ -359,6 +368,10 @@
         push(r0s.at[p], r0r.at[p], r0sem, (p,), other)
         keep = jnp.dot(dlb[pl.ds(ours, half), :], cols, preferred_element_type=jnp.float32)
         own[p] = keep.reshape(4, NX, ROWS, WIDE)
+
+    def send_y(p, r):
+        n, to = y_slot[p], mod(x + ROUNDS[r], NX)
+        push(ys.at[n, :, to], yr.at[n, :, to], ysem, (n, r), at_y(chunks[p][1]))
 
     def pass_on(p):
         kind, i = chunks[p]
@@ -377,7 +390,7 @@
         else:
             n = y_slot[p]
             ys[n] = both.astype(jnp.bfloat16)
-            push(ys.at[n], yr.at[n], ysem, (n,), at_y(i))
+            send_y(p, 0)
 
     compute(0)
     compute(1)
@@ -410,82 +423,91 @@
     pass_on(4)
     pass_on(5)
 
-    for j in range(2):
+    for r in range(1, 4):
+        for p in (0, 2, 4):
+            send_y(p, r)
+
+    def gather_y(r):
+        to = mod(x + ROUNDS[r], NX)
         for n in range(3):
-            landed(xr.at[j, n], xsem, (j, n))
-        got = own[x_at[j], :, x]
+            landed(yr.at[n, :, to], ysem, (n, r))
+        both = own[5, :, to]
         for n in range(3):
-            got += xr[j, n].astype(jnp.float32)
-        for h in range(2):
-            piece = got[:, :, h * NARROW:(h + 1) * NARROW]
-            acc2[2 * j + h] = piece
-            y2s[2 * j + h] = piece.astype(jnp.bfloat16)
-    for n in range(3):
-        to = mod(y + n + 1, NY)
-        push(y2s.at[to], y2r.at[n], y2sem, (n,), at_y(to))
-
+            both += yr[n, :, to].astype(jnp.float32)
+        if r < 3:
+            x2s[:, to] = both.astype(jnp.bfloat16)
+            push(x2s.at[:, to], x2r.at[r], x2sem, (r,), at_x(to))
+        return both
+
+    def gather_x():
+        for j in range(2):
+            for n in range(3):
+                landed(xr.at[j, n], xsem, (j, n))
+            got = own[x_at[j], :, x]
+            for n in range(3):
+                got += xr[j, n].astype(jnp.float32)
+            for h in range(2):
+                piece = got[:, :, h * NARROW:(h + 1) * NARROW]
+                acc2[2 * j + h] = piece
+                y2s[2 * j + h] = piece.astype(jnp.bfloat16)
+        for n in range(3):
+            to = mod(y + n + 1, NY)
+            push(y2s.at[to], y2r.at[n], y2sem, (n,), at_y(to))
+
+    def weight_grads(q):
+        grads = jnp.dot(
+            a2ar[...].reshape(NS * ROWS, TOK),
+            hb[q].reshape(TOK, QUART),
+            preferred_element_type=jnp.float32,
+        )
+        slots_ref[:, q * QUART:(q + 1) * QUART] = grads.astype(jnp.bfloat16)
+
+    z_copies = []
+
+    def send_sections(part, src, dst):
+        for i in range(4):
+            to = 4 * c + i
+            copy = pltpu.make_async_remote_copy(
+                src_ref=src.at[i],
+                dst_ref=dst.at[mod(to - z, NZ)],
+                send_sem=zsem.at[0, part, i],
+                recv_sem=zsem.at[1, part, 0],
+                device_id=at_z(to),
+                device_id_type=MESH,
+            )
+            z_copies.append((to, copy))
+
+            @pl.when(to != z)
+            def _():
+                copy.start()
+
+    gather_y(0)
+    gather_y(1)
+    gather_x()
+    gather_y(2)
     a2ar[sec] = a2as[sec]
     pltpu.make_async_copy(
         a2ar.at[pl.ds(0, NS - 1)], a2ar.at[pl.ds(0, NS - 1)], asem.at[1]
     ).wait()
-    outs = []
-    for q in range(4):
-        if q >= 2:
-            outs[q - 2].wait()
-        grads = jnp.dot(
-            a2ar[...].reshape(NS * ROWS, TOK),
-            hb[q].reshape(TOK, QUART),
-            preferred_element_type=jnp.float32,
-        )
-        stage[q % 2] = grads.astype(jnp.bfloat16)
-        out = pltpu.make_async_copy(
-            stage.at[q % 2], slots_hbm.at[:, q * QUART:(q + 1) * QUART], out_sem.at[q]
-        )
-        out.start()
-        outs.append(out)
-
+    weight_grads(0)
+    weight_grads(1)
+    wide = gather_y(3)
     for n in range(3):
-        landed(yr.at[n], ysem, (n,))
-    both = own[5]
-    for n in range(3):
-        both += yr[n].astype(jnp.float32)
-    own[5] = both
-    x2s[...] = both.astype(jnp.bfloat16)
-    for n, dx in enumerate(DX):
-        to = mod(x + dx, NX)
-        push(x2s.at[:, to], x2r.at[n], x2sem, (n,), at_x(to))
-
+        landed(x2r.at[n], x2sem, (n,))
+        wide += x2r[n].astype(jnp.float32)
+    zf[:, :, :WIDE] = wide
+    zsw[...] = wide.astype(jnp.bfloat16)
+    send_sections(0, zsw, zrw)
+    narrow = acc2[y]
     for n in range(3):
         landed(y2r.at[n], y2sem, (n,))
-    narrow = acc2[y]
-    for n in range(3):
         narrow += y2r[n].astype(jnp.float32)
-    for n in range(3):
-        landed(x2r.at[n], x2sem, (n,))
-    wide = own[5, :, x]
-    for n in range(3):
-        wide += x2r[n].astype(jnp.float32)
-    zf[:, :, :WIDE] = wide
     zf[:, :, WIDE:] = narrow
-    zs[:, :, :WIDE] = wide.astype(jnp.bfloat16)
-    zs[:, :, WIDE:] = narrow.astype(jnp.bfloat16)
+    zsn[...] = narrow.astype(jnp.bfloat16)
+    send_sections(1, zsn, zrn)
+    weight_grads(2)
+    weight_grads(3)
     mine = z // 4 == c
-    z_copies = []
-    for i in range(4):
-        to = 4 * c + i
-        copy = pltpu.make_async_remote_copy(
-            src_ref=zs.at[i],
-            dst_ref=zr.at[mod(to - z, NZ)],
-            send_sem=zsem.at[0, i],
-            recv_sem=zsem.at[1, 0],
-            device_id=at_z(to),
-            device_id_type=MESH,
-        )
-        z_copies.append((to, copy))
-
-        @pl.when(to != z)
-        def _():
-            copy.start()
 
     f_copies = []
     for t in range(NT):
@@ -501,13 +523,15 @@
 
     @pl.when(mine)
     def _():
-        zr[0] = jnp.zeros((ROWS, QUART), jnp.bfloat16)
-        pltpu.make_async_copy(
-            zr.at[pl.ds(1, NZ - 1)], zr.at[pl.ds(1, NZ - 1)], zsem.at[1, 0]
-        ).wait()
-        final = zf[z % 4]
+        for part, got in enumerate((zrw, zrn)):
+            pltpu.make_async_copy(
+                got.at[pl.ds(1, NZ - 1)], got.at[pl.ds(1, NZ - 1)], zsem.at[1, part, 0]
+            ).wait()
+        high, low = zf[z % 4, :, :WIDE], zf[z % 4, :, WIDE:]
         for i in range(1, NZ):
-            final += zr[i].astype(jnp.float32)
+            high += zrw[i].astype(jnp.float32)
+            low += zrn[i].astype(jnp.float32)
+        final = jnp.concatenate([high, low], axis=1)
         for t in range(NT):
             fin_s[t] = final[2 * t:2 * t + 2]
         for t in range(NT):
@@ -544,8 +568,6 @@
     pltpu.make_async_copy(
         a2as.at[pl.ds(0, NS - 1)], a2as.at[pl.ds(0, NS - 1)], asem.at[0]
     ).wait()
-    outs[2].wait()
-    outs[3].wait()
 
 
 def on_device(hidden, head_weight, panel_section, targets):
@@ -558,12 +580,12 @@
         body,
         name="head_step",
         out_shape=(
-            jax.ShapeDtypeStruct((1, TOK), f32),
-            jax.ShapeDtypeStruct((2, D), f32),
-            jax.ShapeDtypeStruct((NS * ROWS, D), bf16),
+            pltpu.VMEM((1, ROWS), f32),
+            pltpu.VMEM((2, D), f32),
+            pltpu.VMEM((NS * ROWS, D), bf16),
         ),
         in_specs=[vmem, hbm, vmem, vmem],
-        out_specs=(vmem, vmem, hbm),
+        out_specs=(vmem, vmem, vmem),
         scratch_shapes=[
             pltpu.VMEM((VOC, D), bf16),
             pltpu.VMEM((4, NZ, NX, ROWS, QUART), bf16),
@@ -573,10 +595,10 @@
             pltpu.VMEM((TOK, 128), f32),
             pltpu.VMEM((NS, ROWS, TOK), bf16),
             pltpu.VMEM((NS, ROWS, TOK), bf16),
-            pltpu.VMEM((3, 8, TOK), f32),
-            pltpu.VMEM((NZ - 1, 8, TOK), f32),
-            pltpu.VMEM((NX - 1, 8, TOK), f32),
-            pltpu.VMEM((NT - 1, 8, TOK), f32),
+            pltpu.VMEM((3, 1, 3 * TOK), f32),
+            pltpu.VMEM((NZ - 1, 1, 3 * TOK), f32),
+            pltpu.VMEM((NX - 1, 1, 3 * TOK), f32),
+            pltpu.VMEM((NT - 1, 1, 3 * TOK), f32),
             pltpu.VMEM((6, 4, NX, ROWS, WIDE), bf16),
             pltpu.VMEM((6, 4, NX, ROWS, WIDE), bf16),
             pltpu.VMEM((6, 4, NX, ROWS, WIDE), f32),
@@ -590,13 +612,13 @@
             pltpu.VMEM((4, 4, ROWS, NARROW), bf16),
             pltpu.VMEM((3, 4, ROWS, NARROW), bf16),
             pltpu.VMEM((4, ROWS, QUART), f32),
-            pltpu.VMEM((4, ROWS, QUART), bf16),
-            pltpu.VMEM((NZ, ROWS, QUART), bf16),
+            pltpu.VMEM((4, ROWS, WIDE), bf16),
+            pltpu.VMEM((4, ROWS, NARROW), bf16),
+            pltpu.VMEM((NZ, ROWS, WIDE), bf16),
+            pltpu.VMEM((NZ, ROWS, NARROW), bf16),
             pltpu.VMEM((NT, 2, QUART), f32),
             pltpu.VMEM((NY, 2, QUART), f32),
-            pltpu.VMEM((2, NS * ROWS, QUART), bf16),
             dma((1,)),
-            dma((4,)),
             dma((2, 2, 4)),
             dma((2, 3, 8)),
             dma((2, 3)),
@@ -605,15 +627,15 @@
             dma((2, 3, 7)),
             dma((2,)),
             dma((2, 6)),
-            dma((2, 3)),
+            dma((2, 3, 4)),
             dma((2, 2, 3)),
             dma((2, 3)),
             dma((2, 3)),
-            dma((2, 4)),
+            dma((2, 2, 4)),
             dma((2, 8)),
         ],
         compiler_params=pltpu.CompilerParams(
-            collective_id=0, has_side_effects=True, vmem_limit_bytes=60 * 2**20
+            collective_id=0, has_side_effects=True, vmem_limit_bytes=48 * 2**20
         ),
     )(
         hidden,
@@ -621,10 +643,7 @@
         panel_section.reshape(1, -1),
         targets.reshape(1, -1),
     )
-    own_rows = hidden.shape[0]
-    myself = lax.axis_index("section")
-    own_loss = lax.dynamic_slice_in_dim(loss[0], myself * own_rows, own_rows)
-    return (own_loss, hidden_grad, grads.reshape(1, NS, 2, rows, width))
+    return (loss.reshape(ROWS), hidden_grad, grads.reshape(1, NS, 2, rows, width))
 
 
 def solution(mesh):

time: 103 us -> 91.8 us (0.89)
  Pallas kernels: 94.9 us -> 85.3 us
  local copies, waits for them, and re-layouts: 7.45 us -> 5.59 us
    pallas_call x1, Pallas kernels: 94.9 us -> 85.3 us  [on_device(): pl.pallas_call(body, name='head_step', out_shape=(pltpu.VMEM((1, ROWS), f...]
    dynamic_slice x1 -> x0, local copies, waits for them, and re-layouts: 1.24 us -> none  [on_device(): own_loss = lax.dynamic_slice_in_dim(loss[0], myself * own_rows, own_rows)]
    unnamed x2 -> x9, local copies, waits for them, and re-layouts: 6.21 us -> 5.59 us
where the time goes in v3:
time: 91.8 us; the launch traced here: 91.6 us
  Pallas kernels  85.3 us (93%)
  local copies, waits for them, and re-layouts  5.59 us (6%)
    pallas_call x1, Pallas kernels, on_device(): pl.pallas_call(body, name='head_step', out_shape=(pltpu.VMEM((1, ROWS), f...  85.3 us
    unnamed x9, local copies, waits for them, and re-layouts  5.59 us

profile of v3, /device:TPU:1, one launch (start us, length us, event | category | flops | bytes accessed | tf_op | source)
XLA Modules:
  0.0 91.6 jit_solution(13583262694157150588)
XLA Ops:
  0.6 0.0 copy-start
  0.6 0.9 copy-done
  1.5 0.0 copy-start.1
  1.5 0.7 copy-done.1
  2.2 0.0 copy-start.2
  2.2 0.7 copy-done.2
  2.9 85.3 %head_step.1 = (f32[1,16]{1,0:T(1,128)S(1)}, f32[2,4608]{1,0:T(2,128)S(1)}, bf16[512,4608]{1,0:T(8,128)(2,1)S(1)}) custom-call(bf16[16,4608]{1,0:T(8,128)(2,1)S(1)} %copy-done, bf16[512,4608]{1,0:T(8,128)(2,1)} %bitcast.9, s32[1,2048]{1,0:T(1,128)S(1)} %bitcast.7, s32[1,512]{1,0:T(1,128)S(1)} %bitcast.8), custom_call_target="tpu_custom_call" | custom-call | tf_op jit(solution)/shard_map/head_step/pallas_call | solution.py:579
  88.3 0.5 copy.10
  88.8 0.6 copy.11
  89.4 2.2 %copy.12 = bf16[1,32,2,8,4608]{4,3,2,1,0:T(8,128)(2,1)} copy(bf16[1,32,2,8,4608]{4,3,2,1,0:T(8,128)(2,1)S(1)} %bitcast.5) | data formatting | bytes 9437184
Async XLA Ops:
  0.6 0.9 copy-start
  1.5 0.7 copy-start.1
  2.2 0.7 copy-start.2

commit v4 on v3

--- a/solution.py
+++ b/solution.py
@@ -15,8 +15,9 @@
 ROWS = 16
 VOC = 512
 QUART = D // 4
-WIDE = 768
-NARROW = 384
+WIDE = 896
+CROSS = 512
+NARROW = 256
 DX = (1, 3, 2)
 ROUNDS = (2, 1, 3, 0)
 NT_DIMS = (((1,), (1,)), ((), ()))
@@ -27,13 +28,15 @@
 
 
 def body(
-    hidden_ref,
+    hidden_hbm,
     weight_hbm,
-    panels_ref,
-    targets_ref,
+    panels_hbm,
+    targets_hbm,
     loss_ref,
     hgrad_ref,
     slots_ref,
+    panels_ref,
+    targets_ref,
     w,
     hb,
     lbuf,
@@ -49,6 +52,10 @@
     r0s,
     r0r,
     own,
+    r0sx,
+    r0rx,
+    ownx,
+    tr,
     ys,
     yr,
     xs,
@@ -66,14 +73,15 @@
     fin_s,
     fin_r,
     local_sem,
-    gz0,
+    gz,
     gx0,
     gx1,
-    gz1,
+    gy1,
     gcore,
     bsem,
     asem,
     r0sem,
+    trsem,
     ysem,
     xsem,
     x2sem,
@@ -115,15 +123,27 @@
     def landed(dst, sems, where):
         pltpu.make_async_copy(dst, dst, sems.at[(1, *where)]).wait()
 
+    own_in = []
+    for part in range(2):
+        for core in range(2):
+            lo = (2 * core + part) * QUART
+            copy = pltpu.make_async_copy(
+                hidden_hbm.at[:, lo:lo + QUART],
+                hb.at[2 * core + part, z, x],
+                local_sem.at[1 + part],
+            )
+            own_in.append((core, copy))
+
+            @pl.when(c == core)
+            def _():
+                copy.start()
+
+    names_in = pltpu.make_async_copy(panels_hbm, panels_ref, local_sem.at[3])
+    names_in.start()
+    targets_in = pltpu.make_async_copy(targets_hbm, targets_ref, local_sem.at[4])
+    targets_in.start()
     w_in = pltpu.make_async_copy(weight_hbm, w, local_sem.at[0])
     w_in.start()
-    for part in range(2):
-        for core in range(2):
-            @pl.when(c == core)
-            def _():
-                lo = (2 * core + part) * QUART
-                hb[2 * core + part, z, x] = hidden_ref[:, lo:lo + QUART]
-
     barrier = pltpu.get_barrier_semaphore()
 
     def greet_sections(i, carry):
@@ -141,9 +161,12 @@
         return carry
 
     lax.fori_loop(1, NT, greet_tensors, 0)
+    for core, copy in own_in:
+        @pl.when(c == core)
+        def _():
+            copy.wait()
+
     pl.semaphore_wait(barrier, NS - 1 + NT - 1)
-
-    fwd, bwd = at_z(mod(z + sgn, NZ)), at_z(mod(z - sgn, NZ))
 
     def back(k):
         return mod(z - k * sgn, NZ)
@@ -151,25 +174,47 @@
     def ahead(k):
         return mod(z + k * sgn, NZ)
 
-    def send_z(q, sems, zz, xx, way, k, *stream):
-        piece = hb.at[q, zz, xx]
-        push(piece, piece, sems, (way, k, *stream), fwd if way == 0 else bwd)
-
-    def send_x(q, sems, zz, *where):
+    order = [z] + [back((n + 1) // 2) if n % 2 else ahead(n // 2) for n in range(1, 8)]
+    streams = [x] + [mod(x - dx, NX) for dx in DX]
+    mine_x = mod(x + y, NX)
+
+    def send_z(part, q, n, xx, to, arrives):
+        piece = hb.at[q, order[n], xx]
+        push(piece, piece, gz, (part, arrives), at_z(order[to]))
+
+    def spread_z(part, q, xx):
+        for to, arrives in ((2, 1), (1, 2), (4, 3), (3, 4)):
+            send_z(part, q, 0, xx, to, arrives)
+
+    def relay_z(part, q, n, xx):
+        landed(hb.at[q, order[n], xx], gz, (part, n))
+        if n == 3:
+            send_z(part, q, 3, xx, 2, 5)
+            send_z(part, q, 3, xx, 4, 7)
+        if n == 4:
+            send_z(part, q, 4, xx, 1, 6)
+
+    def send_x0(n):
+        piece = hb.at[q0, order[n], x]
         for i, dx in enumerate(DX):
-            piece = hb.at[q, zz, x]
-            push(piece, piece, sems, (i, *where), at_x(mod(x + dx, NX)))
-
-    streams = [x] + [mod(x - dx, NX) for dx in DX]
-
-    send_z(q0, gz0, z, x, 0, 0)
-    send_z(q0, gz0, z, x, 1, 0)
-    send_x(q1, gx1, z)
-    send_z(q1, gz1, z, x, 0, 0, 0)
-    send_z(q1, gz1, z, x, 1, 0, 0)
-    send_x(q0, gx0, z, 0)
-
-    w_in.wait()
+            push(piece, piece, gx0, (i, n), at_x(mod(x + dx, NX)))
+
+    def send_y1(n):
+        piece = hb.at[q1, order[n], mine_x]
+        for i in range(3):
+            push(piece, piece, gy1, (i, n), at_y(mod(y + 1 + i, NY)))
+
+    def cross(q, part, n):
+        piece = hb.at[q, order[n]]
+        push(piece, piece, gcore, (part, n), other)
+
+    for i, dx in enumerate(DX):
+        push(hb.at[q1, z, x], hb.at[q1, z, x], gx1, (i,), at_x(mod(x + dx, NX)))
+    spread_z(0, q0, x)
+    send_x0(0)
+
+    names_in.wait()
+    targets_in.wait()
     lane = lax.broadcasted_iota(jnp.int32, (VOC, VOC), 1)
     row = lax.broadcasted_iota(jnp.int32, (VOC, VOC), 0)
     base = pl.multiple_of((sec // 2) * 128, 128)
@@ -193,74 +238,40 @@
     ids = jnp.broadcast_to(targets_ref[...].astype(jnp.float32), (128, TOK))
     tcol[...] = jnp.transpose(ids)
 
-    def step0(k):
-        landed(hb.at[q0, back(k + 1), x], gz0, (0, k))
-        if k < 3:
-            send_z(q0, gz0, back(k + 1), x, 0, k + 1)
-        send_x(q0, gx0, back(k + 1), 2 * k + 1)
-        if k < 3:
-            landed(hb.at[q0, ahead(k + 1), x], gz0, (1, k))
-            if k < 2:
-                send_z(q0, gz0, ahead(k + 1), x, 1, k + 1)
-            send_x(q0, gx0, ahead(k + 1), 2 * k + 2)
-
-    def start1():
-        for i in range(3):
-            landed(hb.at[q1, z, streams[i + 1]], gx1, (i,))
-            send_z(q1, gz1, z, streams[i + 1], 0, 0, i + 1)
-            send_z(q1, gz1, z, streams[i + 1], 1, 0, i + 1)
-        cross(q1, z, 1, 0)
-
-    def step1(k, first, last):
-        for i in range(first, last):
-            xx = streams[i]
-            landed(hb.at[q1, back(k + 1), xx], gz1, (0, k, i))
-            if k < 3:
-                send_z(q1, gz1, back(k + 1), xx, 0, k + 1, i)
-            if k < 3:
-                landed(hb.at[q1, ahead(k + 1), xx], gz1, (1, k, i))
-                if k < 2:
-                    send_z(q1, gz1, ahead(k + 1), xx, 1, k + 1, i)
-        if last == 4:
-            cross(q1, back(k + 1), 1, 2 * k + 1)
-            if k < 3:
-                cross(q1, ahead(k + 1), 1, 2 * k + 2)
-
-    def cross(q, zz, part, n):
-        piece = hb.at[q, zz]
-        push(piece, piece, gcore, (part, n), other)
-
-    order = [z]
-    for k in range(4):
-        order.append(back(k + 1))
-        if k < 3:
-            order.append(ahead(k + 1))
+    def step0(n):
+        relay_z(0, q0, n, x)
+        send_x0(n)
+
+    def step1(n):
+        relay_z(1, q1, n, mine_x)
+        send_y1(n)
 
     def finish0(n):
         for i in range(3):
             landed(hb.at[q0, order[n], streams[i + 1]], gx0, (i, n))
-        cross(q0, order[n], 0, n)
-
-    step0(0)
-    start1()
-    step1(0, 0, 1)
-    step0(1)
-    step1(0, 1, 4)
+        cross(q0, 0, n)
+
+    def finish1(n):
+        for i in range(3):
+            landed(hb.at[q1, order[n], mod(mine_x - 1 - i, NX)], gy1, (i, n))
+        cross(q1, 1, n)
+
+    for i in range(3):
+        landed(hb.at[q1, z, streams[i + 1]], gx1, (i,))
+    spread_z(1, q1, mine_x)
+    cross(q1, 1, 0)
+    for n in (3, 4, 1, 2):
+        step0(n)
+    for n in (3, 4, 1, 2):
+        step1(n)
     finish0(0)
-    step1(1, 0, 1)
-    step0(2)
-    step1(1, 1, 4)
-    finish0(1)
-    finish0(2)
-    step1(2, 0, 1)
-    step0(3)
-    step1(2, 1, 4)
-    finish0(3)
-    finish0(4)
-    step1(3, 0, 4)
-    finish0(5)
-    finish0(6)
-    finish0(7)
+    for n in (5, 6, 7):
+        step0(n)
+    for n in (5, 6, 7):
+        step1(n)
+    for n in range(1, 8):
+        finish0(n)
+        finish1(n)
 
     def logits(first, last):
         for n in range(first, last):
@@ -284,6 +295,7 @@
         for i in range(count):
             lbuf[order[first + i]] = product[i * 64:(i + 1) * 64]
 
+    w_in.wait()
     logits(0, 5)
     logits(5, 8)
 
@@ -345,9 +357,6 @@
     theirs = pl.multiple_of((1 - c) * half, half)
     ours = pl.multiple_of(c * half, half)
 
-    def y_cols(yy):
-        return pl.multiple_of(yy * WIDE, WIDE)
-
     chunks = [
         ("y", mod(y + 2, NY)),
         ("x", 0),
@@ -356,41 +365,60 @@
         ("y", mod(y + 3, NY)),
         ("y", y),
     ]
-    y_slot = {0: 0, 2: 1, 4: 2}
-    x_at = (1, 3)
+    slot = {0: 0, 2: 1, 4: 2, 5: 3}
+
+    def buffers(p):
+        kind, i = chunks[p]
+        if kind == "y":
+            return r0s.at[slot[p]], r0r.at[slot[p]], own.at[slot[p]]
+        return r0sx.at[i], r0rx.at[i], ownx.at[i]
 
     def compute(p):
         kind, i = chunks[p]
-        lo = y_cols(i) if kind == "y" else NY * WIDE + i * WIDE
-        cols = w[:, pl.ds(lo, WIDE)]
+        wide = WIDE if kind == "y" else CROSS
+        lo = pl.multiple_of(i * WIDE, 128) if kind == "y" else NY * WIDE + i * CROSS
+        give_ref, got_ref, keep_ref = buffers(p)
+        cols = w[:, pl.ds(lo, wide)]
         give = jnp.dot(dlb[pl.ds(theirs, half), :], cols, preferred_element_type=jnp.float32)
-        r0s[p] = give.astype(jnp.bfloat16).reshape(4, NX, ROWS, WIDE)
-        push(r0s.at[p], r0r.at[p], r0sem, (p,), other)
+        give_ref[...] = give.astype(jnp.bfloat16).reshape(4, NX, ROWS, wide)
+        push(give_ref, got_ref, r0sem, (p,), other)
         keep = jnp.dot(dlb[pl.ds(ours, half), :], cols, preferred_element_type=jnp.float32)
-        own[p] = keep.reshape(4, NX, ROWS, WIDE)
-
-    def send_y(p, r):
-        n, to = y_slot[p], mod(x + ROUNDS[r], NX)
-        push(ys.at[n, :, to], yr.at[n, :, to], ysem, (n, r), at_y(chunks[p][1]))
+        keep_ref[...] = keep.reshape(4, NX, ROWS, wide)
+
+    def group(r):
+        return mod(x + ROUNDS[r], NX)
+
+    def send_over(r):
+        to = at_y(mod(y + (1 if r % 2 == 0 else 3), NY))
+        push(ys.at[0, :, group(r)], tr.at[r], trsem, (r,), to)
+
+    def send_y(n, r):
+        piece = own[n, :, group(r)]
+        if (n == 1) == (r % 2 == 0):
+            landed(tr.at[r], trsem, (r,))
+            piece += tr[r].astype(jnp.float32)
+        ys[n, :, group(r)] = piece.astype(jnp.bfloat16)
+        to = at_y(mod(y + (1 if n == 1 else 3), NY))
+        push(ys.at[n, :, group(r)], yr.at[n - 1, :, group(r)], ysem, (n - 1, r), to)
 
     def pass_on(p):
         kind, i = chunks[p]
-        landed(r0r.at[p], r0sem, (p,))
-        both = own[p] + r0r[p].astype(jnp.float32)
+        _, got_ref, keep_ref = buffers(p)
+        landed(got_ref, r0sem, (p,))
+        both = keep_ref[...] + got_ref[...].astype(jnp.float32)
+        if p == 0:
+            ys[0] = both.astype(jnp.bfloat16)
+            send_over(0)
+            send_over(1)
+            return
+        keep_ref[...] = both
         if kind == "x":
-            own[p] = both
             xs[i] = both.astype(jnp.bfloat16)
             for n, dx in enumerate(DX):
                 push(
                     xs.at[i, :, mod(x + dx, NX)], xr.at[i, n], xsem, (i, n),
                     at_x(mod(x + dx, NX)),
                 )
-        elif p == 5:
-            own[p] = both
-        else:
-            n = y_slot[p]
-            ys[n] = both.astype(jnp.bfloat16)
-            send_y(p, 0)
 
     compute(0)
     compute(1)
@@ -413,26 +441,31 @@
         return carry
 
     lax.fori_loop(1, NS, scatter, 0)
+    compute(4)
+    pass_on(1)
+    send_over(2)
+    send_over(3)
     compute(2)
-    pass_on(1)
+    pass_on(4)
+    send_y(2, 0)
     compute(3)
     pass_on(2)
-    compute(4)
+    send_y(1, 0)
+    send_y(2, 1)
+    send_y(1, 1)
+    compute(5)
     pass_on(3)
-    compute(5)
-    pass_on(4)
     pass_on(5)
-
-    for r in range(1, 4):
-        for p in (0, 2, 4):
-            send_y(p, r)
+    send_y(2, 2)
+    send_y(1, 2)
+    send_y(2, 3)
+    send_y(1, 3)
 
     def gather_y(r):
-        to = mod(x + ROUNDS[r], NX)
-        for n in range(3):
+        to = group(r)
+        both = own[3, :, to]
+        for n in range(2):
             landed(yr.at[n, :, to], ysem, (n, r))
-        both = own[5, :, to]
-        for n in range(3):
             both += yr[n, :, to].astype(jnp.float32)
         if r < 3:
             x2s[:, to] = both.astype(jnp.bfloat16)
@@ -443,7 +476,7 @@
         for j in range(2):
             for n in range(3):
                 landed(xr.at[j, n], xsem, (j, n))
-            got = own[x_at[j], :, x]
+            got = ownx[j, :, x]
             for n in range(3):
                 got += xr[j, n].astype(jnp.float32)
             for h in range(2):
@@ -491,6 +524,13 @@
     ).wait()
     weight_grads(0)
     weight_grads(1)
+    narrow = acc2[y]
+    for n in range(3):
+        landed(y2r.at[n], y2sem, (n,))
+        narrow += y2r[n].astype(jnp.float32)
+    zf[:, :, WIDE:] = narrow
+    zsn[...] = narrow.astype(jnp.bfloat16)
+    send_sections(1, zsn, zrn)
     wide = gather_y(3)
     for n in range(3):
         landed(x2r.at[n], x2sem, (n,))
@@ -498,13 +538,6 @@
     zf[:, :, :WIDE] = wide
     zsw[...] = wide.astype(jnp.bfloat16)
     send_sections(0, zsw, zrw)
-    narrow = acc2[y]
-    for n in range(3):
-        landed(y2r.at[n], y2sem, (n,))
-        narrow += y2r[n].astype(jnp.float32)
-    zf[:, :, WIDE:] = narrow
-    zsn[...] = narrow.astype(jnp.bfloat16)
-    send_sections(1, zsn, zrn)
     weight_grads(2)
     weight_grads(3)
     mine = z // 4 == c
@@ -574,7 +607,7 @@
     per_section, rows, width = head_weight.shape
     bf16, f32 = jnp.bfloat16, jnp.float32
     vmem = pl.BlockSpec(memory_space=pltpu.VMEM)
-    hbm = pl.BlockSpec(memory_space=pl.ANY)
+    hbm = pl.BlockSpec(memory_space=pltpu.HBM)
     dma = pltpu.SemaphoreType.DMA
     loss, hidden_grad, grads = pl.pallas_call(
         body,
@@ -584,9 +617,11 @@
             pltpu.VMEM((2, D), f32),
             pltpu.VMEM((NS * ROWS, D), bf16),
         ),
-        in_specs=[vmem, hbm, vmem, vmem],
+        in_specs=[hbm, hbm, hbm, hbm],
         out_specs=(vmem, vmem, vmem),
         scratch_shapes=[
+            pltpu.VMEM((1, NS * 64), jnp.int32),
+            pltpu.VMEM((1, TOK), jnp.int32),
             pltpu.VMEM((VOC, D), bf16),
             pltpu.VMEM((4, NZ, NX, ROWS, QUART), bf16),
             pltpu.VMEM((NZ, 64, VOC), f32),
@@ -599,13 +634,17 @@
             pltpu.VMEM((NZ - 1, 1, 3 * TOK), f32),
             pltpu.VMEM((NX - 1, 1, 3 * TOK), f32),
             pltpu.VMEM((NT - 1, 1, 3 * TOK), f32),
-            pltpu.VMEM((6, 4, NX, ROWS, WIDE), bf16),
-            pltpu.VMEM((6, 4, NX, ROWS, WIDE), bf16),
-            pltpu.VMEM((6, 4, NX, ROWS, WIDE), f32),
-            pltpu.VMEM((3, 4, NX, ROWS, WIDE), bf16),
+            pltpu.VMEM((4, 4, NX, ROWS, WIDE), bf16),
+            pltpu.VMEM((4, 4, NX, ROWS, WIDE), bf16),
+            pltpu.VMEM((4, 4, NX, ROWS, WIDE), f32),
+            pltpu.VMEM((2, 4, NX, ROWS, CROSS), bf16),
+            pltpu.VMEM((2, 4, NX, ROWS, CROSS), bf16),
+            pltpu.VMEM((2, 4, NX, ROWS, CROSS), f32),
+            pltpu.VMEM((4, 4, ROWS, WIDE), bf16),
             pltpu.VMEM((3, 4, NX, ROWS, WIDE), bf16),
             pltpu.VMEM((2, 4, NX, ROWS, WIDE), bf16),
-            pltpu.VMEM((2, 3, 4, ROWS, WIDE), bf16),
+            pltpu.VMEM((2, 4, NX, ROWS, CROSS), bf16),
+            pltpu.VMEM((2, 3, 4, ROWS, CROSS), bf16),
             pltpu.VMEM((4, NX, ROWS, WIDE), bf16),
             pltpu.VMEM((3, 4, ROWS, WIDE), bf16),
             pltpu.VMEM((4, 4, ROWS, NARROW), f32),
@@ -618,16 +657,17 @@
             pltpu.VMEM((NZ, ROWS, NARROW), bf16),
             pltpu.VMEM((NT, 2, QUART), f32),
             pltpu.VMEM((NY, 2, QUART), f32),
-            dma((1,)),
-            dma((2, 2, 4)),
+            dma((5,)),
+            dma((2, 2, 8)),
             dma((2, 3, 8)),
             dma((2, 3)),
-            dma((2, 2, 4, 4)),
+            dma((2, 3, 8)),
             dma((2, 2, 8)),
             dma((2, 3, 7)),
             dma((2,)),
             dma((2, 6)),
-            dma((2, 3, 4)),
+            dma((2, 4)),
+            dma((2, 2, 4)),
             dma((2, 2, 3)),
             dma((2, 3)),
             dma((2, 3)),
@@ -638,10 +678,15 @@
             collective_id=0, has_side_effects=True, vmem_limit_bytes=48 * 2**20
         ),
     )(
-        hidden,
-        head_weight.reshape(per_section * rows, width),
-        panel_section.reshape(1, -1),
-        targets.reshape(1, -1),
+        *(
+            pltpu.with_memory_space_constraint(array, pltpu.HBM)
+            for array in (
+                hidden,
+                head_weight.reshape(per_section * rows, width),
+                panel_section.reshape(1, -1),
+                targets.reshape(1, -1),
+            )
+        )
     )
     return (loss.reshape(ROWS), hidden_grad, grads.reshape(1, NS, 2, rows, width))
 

time: 91.8 us -> 86.9 us (0.947)
  Pallas kernels: 85.3 us -> 82.9 us
  local copies, waits for them, and re-layouts: 5.59 us -> 3.31 us
    pallas_call x1, Pallas kernels: 85.3 us -> 82.9 us  [on_device(): pl.pallas_call(body, name='head_step', out_shape=(pltpu.VMEM((1, ROWS), f...]
    unnamed x9 -> x3, local copies, waits for them, and re-layouts: 5.59 us -> 3.31 us
where the time goes in v4:
time: 86.9 us; the launch traced here: 86.8 us
  Pallas kernels  82.9 us (95%)
  local copies, waits for them, and re-layouts  3.31 us (4%)
    pallas_call x1, Pallas kernels, on_device(): pl.pallas_call(body, name='head_step', out_shape=(pltpu.VMEM((1, ROWS), f...  82.9 us
    unnamed x3, local copies, waits for them, and re-layouts  3.31 us

profile of v4, /device:TPU:1, one launch (start us, length us, event | category | flops | bytes accessed | tf_op | source)
XLA Modules:
  0.0 86.8 jit_solution(5611984660613479027)
XLA Ops:
  0.6 82.9 %head_step.1 = (f32[1,16]{1,0:T(1,128)S(1)}, f32[2,4608]{1,0:T(2,128)S(1)}, bf16[512,4608]{1,0:T(8,128)(2,1)S(1)}) custom-call(bf16[16,4608]{1,0:T(8,128)(2,1)} %hidden_hbm.1, bf16[512,4608]{1,0:T(8,128)(2,1)} %bitcast.7, s32[1,2048]{1,0:T(1,128)} %bitcast.8, s32[1,512]{1,0:T(1,128)} %bitcast.9), custom_call_target="tpu_custom_call" | custom-call | tf_op jit(solution)/shard_map/head_step/pallas_call | solution.py:612
  83.5 0.5 copy.10
  84.0 0.6 copy.11
  84.7 2.2 %copy.12 = bf16[1,32,2,8,4608]{4,3,2,1,0:T(8,128)(2,1)} copy(bf16[1,32,2,8,4608]{4,3,2,1,0:T(8,128)(2,1)S(1)} %bitcast.5) | data formatting | bytes 9437184

commit v5 on v4

--- a/solution.py
+++ b/solution.py
@@ -15,6 +15,8 @@
 ROWS = 16
 VOC = 512
 QUART = D // 4
+PIECES = 4
+PARTS = (1280, 1024)
 WIDE = 896
 CROSS = 512
 NARROW = 256
@@ -38,6 +40,7 @@
     panels_ref,
     targets_ref,
     w,
+    ha,
     hb,
     lbuf,
     dlb,
@@ -94,7 +97,7 @@
     z, x = sec // NX, sec % NX
     y, c = ten // NC, ten % NC
     sgn = 1 - 2 * c
-    q0, q1 = 2 * c, 2 * c + 1
+    hbs = (ha, hb)
 
     def at_z(zz):
         return (zz * NX + x, ten)
@@ -120,16 +123,21 @@
         copy.start()
         sent.append(copy)
 
+    def drain(count):
+        for copy in sent[:count]:
+            copy.wait_send()
+        del sent[:count]
+
     def landed(dst, sems, where):
         pltpu.make_async_copy(dst, dst, sems.at[(1, *where)]).wait()
 
     own_in = []
     for part in range(2):
         for core in range(2):
-            lo = (2 * core + part) * QUART
+            lo = core * D // 2 + part * PARTS[0]
             copy = pltpu.make_async_copy(
-                hidden_hbm.at[:, lo:lo + QUART],
-                hb.at[2 * core + part, z, x],
+                hidden_hbm.at[:, lo:lo + PARTS[part]],
+                hbs[part].at[core, z, x],
                 local_sem.at[1 + part],
             )
             own_in.append((core, copy))
@@ -178,39 +186,39 @@
     streams = [x] + [mod(x - dx, NX) for dx in DX]
     mine_x = mod(x + y, NX)
 
-    def send_z(part, q, n, xx, to, arrives):
-        piece = hb.at[q, order[n], xx]
+    def send_z(part, n, xx, to, arrives):
+        piece = hbs[part].at[c, order[n], xx]
         push(piece, piece, gz, (part, arrives), at_z(order[to]))
 
-    def spread_z(part, q, xx):
+    def spread_z(part, xx):
         for to, arrives in ((2, 1), (1, 2), (4, 3), (3, 4)):
-            send_z(part, q, 0, xx, to, arrives)
-
-    def relay_z(part, q, n, xx):
-        landed(hb.at[q, order[n], xx], gz, (part, n))
+            send_z(part, 0, xx, to, arrives)
+
+    def relay_z(part, n, xx):
+        landed(hbs[part].at[c, order[n], xx], gz, (part, n))
         if n == 3:
-            send_z(part, q, 3, xx, 2, 5)
-            send_z(part, q, 3, xx, 4, 7)
+            send_z(part, 3, xx, 2, 5)
+            send_z(part, 3, xx, 4, 7)
         if n == 4:
-            send_z(part, q, 4, xx, 1, 6)
+            send_z(part, 4, xx, 1, 6)
 
     def send_x0(n):
-        piece = hb.at[q0, order[n], x]
+        piece = ha.at[c, order[n], x]
         for i, dx in enumerate(DX):
             push(piece, piece, gx0, (i, n), at_x(mod(x + dx, NX)))
 
     def send_y1(n):
-        piece = hb.at[q1, order[n], mine_x]
+        piece = hb.at[c, order[n], mine_x]
         for i in range(3):
             push(piece, piece, gy1, (i, n), at_y(mod(y + 1 + i, NY)))
 
-    def cross(q, part, n):
-        piece = hb.at[q, order[n]]
+    def cross(part, n):
+        piece = hbs[part].at[c, order[n]]
         push(piece, piece, gcore, (part, n), other)
 
     for i, dx in enumerate(DX):
-        push(hb.at[q1, z, x], hb.at[q1, z, x], gx1, (i,), at_x(mod(x + dx, NX)))
-    spread_z(0, q0, x)
+        push(hb.at[c, z, x], hb.at[c, z, x], gx1, (i,), at_x(mod(x + dx, NX)))
+    spread_z(0, x)
     send_x0(0)
 
     names_in.wait()
@@ -239,27 +247,27 @@
     tcol[...] = jnp.transpose(ids)
 
     def step0(n):
-        relay_z(0, q0, n, x)
+        relay_z(0, n, x)
         send_x0(n)
 
     def step1(n):
-        relay_z(1, q1, n, mine_x)
+        relay_z(1, n, mine_x)
         send_y1(n)
 
     def finish0(n):
         for i in range(3):
-            landed(hb.at[q0, order[n], streams[i + 1]], gx0, (i, n))
-        cross(q0, 0, n)
+            landed(ha.at[c, order[n], streams[i + 1]], gx0, (i, n))
+        cross(0, n)
 
     def finish1(n):
         for i in range(3):
-            landed(hb.at[q1, order[n], mod(mine_x - 1 - i, NX)], gy1, (i, n))
-        cross(q1, 1, n)
+            landed(hb.at[c, order[n], mod(mine_x - 1 - i, NX)], gy1, (i, n))
+        cross(1, n)
 
     for i in range(3):
-        landed(hb.at[q1, z, streams[i + 1]], gx1, (i,))
-    spread_z(1, q1, mine_x)
-    cross(q1, 1, 0)
+        landed(hb.at[c, z, streams[i + 1]], gx1, (i,))
+    spread_z(1, mine_x)
+    cross(1, 0)
     for n in (3, 4, 1, 2):
         step0(n)
     for n in (3, 4, 1, 2):
@@ -277,15 +285,19 @@
         for n in range(first, last):
             mirror = n if n in (0, 7) else (n + 1 if n % 2 else n - 1)
             for part in range(2):
-                landed(hb.at[2 - 2 * c + part, order[n]], gcore, (part, mirror))
+                landed(hbs[part].at[1 - c, order[n]], gcore, (part, mirror))
         count = last - first
         left = jnp.concatenate(
             [
                 jnp.concatenate(
-                    [hb[q, order[n]].reshape(64, QUART) for n in range(first, last)],
+                    [
+                        hbs[part][core, order[n]].reshape(64, PARTS[part])
+                        for n in range(first, last)
+                    ],
                     axis=0,
                 )
-                for q in range(4)
+                for core in range(NC)
+                for part in range(2)
             ],
             axis=1,
         )
@@ -328,7 +340,7 @@
     def share(mine, phase, got, count, device):
         for n in range(3):
             st_s[phase, :, n * TOK:(n + 1) * TOK] = mine[n]
-        for i in range(1, count):
+        for i in sorted(range(1, count), key=lambda i: abs(i - count // 2)):
             push(st_s.at[phase], got.at[i - 1], bsem, (phase, i - 1), device(i))
         for i in range(1, count):
             landed(got.at[i - 1], bsem, (phase, i - 1))
@@ -343,8 +355,6 @@
     best, total, picked = share(
         mine3, 2, st_t, NT, lambda i: (sec, mod(ten + i, NT))
     )
-    loss = jnp.broadcast_to(jnp.log(total) + best - picked, (8, TOK))
-    loss_ref[...] = pltpu.roll(loss, TOK - sec * ROWS, 1)[:1, :ROWS]
     back_cols = jnp.transpose(
         jnp.concatenate(
             [rows8(best, 1.0 / total, picked), jnp.zeros((120, TOK), jnp.float32)], axis=0
@@ -353,6 +363,7 @@
     dl = jnp.exp(scores - back_cols[:, :1]) * back_cols[:, 1:2]
     dlb[...] = (dl - jnp.where(hits, 1.0, 0.0)).astype(jnp.bfloat16)
 
+    early = len(sent)
     half = TOK // 2
     theirs = pl.multiple_of((1 - c) * half, half)
     ours = pl.multiple_of(c * half, half)
@@ -487,13 +498,15 @@
             to = mod(y + n + 1, NY)
             push(y2s.at[to], y2r.at[n], y2sem, (n,), at_y(to))
 
-    def weight_grads(q):
+    def weight_grads(core, part):
+        wide = PARTS[part]
         grads = jnp.dot(
             a2ar[...].reshape(NS * ROWS, TOK),
-            hb[q].reshape(TOK, QUART),
+            hbs[part][core].reshape(TOK, wide),
             preferred_element_type=jnp.float32,
         )
-        slots_ref[:, q * QUART:(q + 1) * QUART] = grads.astype(jnp.bfloat16)
+        lo = core * D // 2 + part * PARTS[0]
+        slots_ref[:, lo:lo + wide] = grads.astype(jnp.bfloat16)
 
     z_copies = []
 
@@ -514,6 +527,9 @@
             def _():
                 copy.start()
 
+    drain(early)
+    loss = jnp.broadcast_to(jnp.log(total) + best - picked, (8, TOK))
+    loss_ref[...] = pltpu.roll(loss, TOK - sec * ROWS, 1)[:1, :ROWS]
     gather_y(0)
     gather_y(1)
     gather_x()
@@ -522,8 +538,8 @@
     pltpu.make_async_copy(
         a2ar.at[pl.ds(0, NS - 1)], a2ar.at[pl.ds(0, NS - 1)], asem.at[1]
     ).wait()
-    weight_grads(0)
-    weight_grads(1)
+    weight_grads(0, 0)
+    weight_grads(0, 1)
     narrow = acc2[y]
     for n in range(3):
         landed(y2r.at[n], y2sem, (n,))
@@ -538,8 +554,12 @@
     zf[:, :, :WIDE] = wide
     zsw[...] = wide.astype(jnp.bfloat16)
     send_sections(0, zsw, zrw)
-    weight_grads(2)
-    weight_grads(3)
+    weight_grads(1, 0)
+    weight_grads(1, 1)
+    drain(len(sent))
+    pltpu.make_async_copy(
+        a2as.at[pl.ds(0, NS - 1)], a2as.at[pl.ds(0, NS - 1)], asem.at[0]
+    ).wait()
     mine = z // 4 == c
 
     f_copies = []
@@ -574,6 +594,11 @@
 
         fin_r[y] = fin_s[ten]
 
+    for to, copy in z_copies:
+        @pl.when(to != z)
+        def _():
+            copy.wait_send()
+
     for i in range(NY):
         @pl.when(jnp.logical_not(mine & (y == i)))
         def _():
@@ -591,16 +616,23 @@
             def _():
                 f_copies[t].wait_send()
 
-    for to, copy in z_copies:
-        @pl.when(to != z)
-        def _():
-            copy.wait_send()
-
-    for copy in sent:
-        copy.wait_send()
-    pltpu.make_async_copy(
-        a2as.at[pl.ds(0, NS - 1)], a2as.at[pl.ds(0, NS - 1)], asem.at[0]
-    ).wait()
+
+def write_out(loss_ref, hgrad_ref, slots_ref, loss_hbm, hgrad_hbm, slots_hbm, sems):
+    rows = NS * ROWS // PIECES
+    copies = [
+        pltpu.make_async_copy(
+            slots_ref.at[i * rows:(i + 1) * rows],
+            slots_hbm.at[i * rows:(i + 1) * rows],
+            sems.at[2 + i],
+        )
+        for i in range(PIECES)
+    ]
+    copies.append(pltpu.make_async_copy(loss_ref, loss_hbm, sems.at[0]))
+    copies.append(pltpu.make_async_copy(hgrad_ref, hgrad_hbm, sems.at[1]))
+    for copy in copies:
+        copy.start()
+    for copy in copies:
+        copy.wait()
 
 
 def on_device(hidden, head_weight, panel_section, targets):
@@ -623,7 +655,8 @@
             pltpu.VMEM((1, NS * 64), jnp.int32),
             pltpu.VMEM((1, TOK), jnp.int32),
             pltpu.VMEM((VOC, D), bf16),
-            pltpu.VMEM((4, NZ, NX, ROWS, QUART), bf16),
+            pltpu.VMEM((NC, NZ, NX, ROWS, PARTS[0]), bf16),
+            pltpu.VMEM((NC, NZ, NX, ROWS, PARTS[1]), bf16),
             pltpu.VMEM((NZ, 64, VOC), f32),
             pltpu.VMEM((TOK, VOC), bf16),
             pltpu.VMEM((VOC, VOC), bf16),
@@ -688,6 +721,24 @@
             )
         )
     )
+    loss, hidden_grad, grads = pl.pallas_call(
+        write_out,
+        name="write_out",
+        out_shape=(
+            jax.ShapeDtypeStruct((1, ROWS), f32),
+            jax.ShapeDtypeStruct((2, D), f32),
+            jax.ShapeDtypeStruct((NS * ROWS, D), bf16),
+        ),
+        in_specs=[vmem] * 3,
+        out_specs=(hbm, hbm, hbm),
+        scratch_shapes=[dma((2 + PIECES,))],
+        compiler_params=pltpu.CompilerParams(vmem_limit_bytes=2 * 2**20),
+    )(
+        *(
+            pltpu.with_memory_space_constraint(array, pltpu.VMEM)
+            for array in (loss, hidden_grad, grads)
+        )
+    )
     return (loss.reshape(ROWS), hidden_grad, grads.reshape(1, NS, 2, rows, width))
 
 

time: 86.9 us -> 83.9 us (0.965)
  local copies, waits for them, and re-layouts: 3.31 us -> 0 us
    unnamed x3 -> x0, local copies, waits for them, and re-layouts: 3.31 us -> none
    pallas_call x0 -> x1, Pallas kernels: none -> 2.24 us  [on_device(): pl.pallas_call(write_out, name='write_out', out_shape=(jax.ShapeDtypeStru...]
    pallas_call x1, Pallas kernels: 82.9 us -> 81 us  [on_device(): pl.pallas_call(body, name='head_step', out_shape=(pltpu.VMEM((1, ROWS), f...]
where the time goes in v5:
time: 83.9 us; the launch traced here: 83.8 us
  Pallas kernels  83.2 us (99%)
    pallas_call x1, Pallas kernels, on_device(): pl.pallas_call(body, name='head_step', out_shape=(pltpu.VMEM((1, ROWS), f...  81 us
    pallas_call x1, Pallas kernels, on_device(): pl.pallas_call(write_out, name='write_out', out_shape=(jax.ShapeDtypeStru...  2.24 us

profile of v5, /device:TPU:1, one launch (start us, length us, event | category | flops | bytes accessed | tf_op | source)
XLA Modules:
  0.0 83.8 jit_solution(729423261861705718)
XLA Ops:
  0.6 81.0 %head_step.1 = (f32[1,16]{1,0:T(1,128)S(1)}, f32[2,4608]{1,0:T(2,128)S(1)}, bf16[512,4608]{1,0:T(8,128)(2,1)S(1)}) custom-call(bf16[16,4608]{1,0:T(8,128)(2,1)} %hidden_hbm.1, bf16[512,4608]{1,0:T(8,128)(2,1)} %bitcast.5, s32[1,2048]{1,0:T(1,128)} %bitcast.6, s32[1,512]{1,0:T(1,128)} %bitcast.7), custom_call_target="tpu_custom_call" | custom-call | tf_op jit(solution)/shard_map/head_step/pallas_call | solution.py:644
  81.6 2.2 %write_out.1 = (f32[1,16]{1,0:T(1,128)}, f32[2,4608]{1,0:T(2,128)}, bf16[512,4608]{1,0:T(8,128)(2,1)}) custom-call(f32[1,16]{1,0:T(1,128)S(1)} %get-tuple-element.9.loss_ref, f32[2,4608]{1,0:T(2,128)S(1)} %get-tuple-element.10.hgrad_ref, bf16[512,4608]{1,0:T(8,128)(2,1)S(1)} %get-tuple-element.11.slots_ref), custom_call_target="tpu_custom_call" | custom-call | tf_op jit(solution)/shard_map/write_out/pallas_call | solution.py:724

commit v6 on v5

--- a/solution.py
+++ b/solution.py
@@ -432,8 +432,6 @@
                 )
 
     compute(0)
-    compute(1)
-    pass_on(0)
     packed = lax.dot_general(
         pack[...], dlb[...], NT_DIMS, preferred_element_type=jnp.float32
     )
@@ -452,6 +450,8 @@
         return carry
 
     lax.fori_loop(1, NS, scatter, 0)
+    compute(1)
+    pass_on(0)
     compute(4)
     pass_on(1)
     send_over(2)

time: 83.9 us -> 82.4 us (0.982)
  Pallas kernels: 83.2 us -> 81.5 us
    pallas_call x1, Pallas kernels: 81 us -> 79.2 us  [on_device(): pl.pallas_call(body, name='head_step', out_shape=(pltpu.VMEM((1, ROWS), f...]
where the time goes in v6:
time: 82.4 us; the launch traced here: 82.1 us
  Pallas kernels  81.5 us (99%)
    pallas_call x1, Pallas kernels, on_device(): pl.pallas_call(body, name='head_step', out_shape=(pltpu.VMEM((1, ROWS), f...  79.2 us
    pallas_call x1, Pallas kernels, on_device(): pl.pallas_call(write_out, name='write_out', out_shape=(jax.ShapeDtypeStru...  2.24 us

profile of v6, /device:TPU:1, one launch (start us, length us, event | category | flops | bytes accessed | tf_op | source)
XLA Modules:
  0.0 82.1 jit_solution(3511992925833400881)
XLA Ops:
  0.6 79.2 %head_step.1 = (f32[1,16]{1,0:T(1,128)S(1)}, f32[2,4608]{1,0:T(2,128)S(1)}, bf16[512,4608]{1,0:T(8,128)(2,1)S(1)}) custom-call(bf16[16,4608]{1,0:T(8,128)(2,1)} %hidden_hbm.1, bf16[512,4608]{1,0:T(8,128)(2,1)} %bitcast.5, s32[1,2048]{1,0:T(1,128)} %bitcast.6, s32[1,512]{1,0:T(1,128)} %bitcast.7), custom_call_target="tpu_custom_call" | custom-call | tf_op jit(solution)/shard_map/head_step/pallas_call | solution.py:644
  79.9 2.2 %write_out.1 = (f32[1,16]{1,0:T(1,128)}, f32[2,4608]{1,0:T(2,128)}, bf16[512,4608]{1,0:T(8,128)(2,1)}) custom-call(f32[1,16]{1,0:T(1,128)S(1)} %get-tuple-element.9.loss_ref, f32[2,4608]{1,0:T(2,128)S(1)} %get-tuple-element.10.hgrad_ref, bf16[512,4608]{1,0:T(8,128)(2,1)S(1)} %get-tuple-element.11.slots_ref), custom_call_target="tpu_custom_call" | custom-call | tf_op jit(solution)/shard_map/write_out/pallas_call | solution.py:724
